TPU v7x, 256 devices: a whole 4x4x8 slice. The times are simulated.
256 devices in a mesh: ctx: 32 (over y, x, core), head: 8 (over z).
Axes of the slice: x: 4, y: 4, z: 8, core: 2. Of those that a mesh axis runs over, the one named last changes fastest.
Arguments:
- queries: bfloat16 [4096, 8192], P('ctx', 'head'), parts along dimension 1, may hold values from -5 to 5
- keys: bfloat16 [4096, 1024], P('ctx', 'head'), parts along dimension 1, may hold values from -5 to 5
- values: bfloat16 [4096, 1024], P('ctx', 'head'), parts along dimension 1, may hold values from -6 to 6
- grad_out: bfloat16 [4096, 8192], P('ctx', 'head'), parts along dimension 1, may hold values from -6 to 6
- doc_lengths: int32 [4], replicated, may hold values from 1 to 2048, 4096 in all
- stretch_order: int32 [64], replicated, may hold values from 0 to 63, each once
Outputs:
- grad_queries: bfloat16 [4096, 8192], P('ctx', 'head'), parts along dimension 1
- grad_keys: bfloat16 [4096, 1024], P('ctx', 'head'), parts along dimension 1
- grad_values: bfloat16 [4096, 1024], P('ctx', 'head'), parts along dimension 1
There are 8 independent parts, one for each index of `head`. A program takes and returns all parts, laid end to end along the dimension named above; an argument that names none is the same for every part. Nothing has to cross between parts.
Inputs may be any that keep to these rules, and one draw needn't show every extreme that they name: `doc_lengths`: the lengths sum to 4096; the longest is exactly 2048. `stretch_order`: each stretch number appears exactly once.
All inputs are finite; a program needn't handle non-finite values.
Results may differ from a plain program's by a relative error of at most 0.018.
Values may be sent and summed in bfloat16 or wider, within the bound.
A program may use at most 64 MiB of HBM per device.

v0:
```python
import jax
import jax.numpy as jnp
from jax import lax
from jax.sharding import PartitionSpec as P


def body(queries, keys, values, grad_out, doc_lengths, stretch_order):
    row_count, feature_width = queries.shape
    head_dim = keys.shape[1]
    head_count = feature_width // head_dim
    all_rows = row_count * lax.axis_size("ctx")
    stretch_rows = row_count // 2
    scaling = head_dim ** (-0.5)
    key_rows = min(512, all_rows)
    block_count = all_rows // key_rows
    row_index = jnp.arange(all_rows, dtype=jnp.int32)
    positions = stretch_order[row_index // stretch_rows] * stretch_rows + row_index % stretch_rows
    starts = jnp.cumsum(doc_lengths) - doc_lengths
    my_begin = lax.axis_index("ctx") * row_count
    my_pos = lax.dynamic_slice_in_dim(positions, my_begin, row_count, 0)
    inside = starts[None, :] <= my_pos[:, None]
    my_first = jnp.max(jnp.where(inside, starts[None, :], 0), axis=1)
    gathered_keys, gathered_values = (
        lax.all_gather(keys, "ctx", axis=0, tiled=True),
        lax.all_gather(values, "ctx", axis=0, tiled=True),
    )
    query_heads = queries.reshape(row_count, head_count, head_dim)
    grad_heads = grad_out.reshape(row_count, head_count, head_dim)
    grad_wide = grad_heads.astype(jnp.float32)

    def block_view(first_row, span_rows):
        key_pos = lax.dynamic_slice_in_dim(positions, first_row, span_rows, 0)
        allowed = (key_pos[None, :] <= my_pos[:, None]) & (key_pos[None, :] >= my_first[:, None])
        key_block = lax.dynamic_slice_in_dim(gathered_keys, first_row, span_rows, 0)
        value_block = lax.dynamic_slice_in_dim(gathered_values, first_row, span_rows, 0)
        return (allowed, key_block, value_block)

    def score_block(key_block):
        return (
            jnp.einsum("rhd,kd->hrk", query_heads, key_block, preferred_element_type=jnp.float32)
            * scaling
        )

    def stat_step(running, block_index):
        allowed, key_block, value_block = block_view(block_index * key_rows, key_rows)

        def stat_update(running_state):
            row_max, row_sum = running_state
            scores = score_block(key_block)
            newest = jnp.maximum(
                row_max, jnp.max(jnp.where(allowed[None], scores, -jnp.inf), axis=2)
            )
            shifted = jnp.where(jnp.isfinite(newest), newest, 0.0)
            new_sum = row_sum * jnp.exp(row_max - shifted)
            new_sum = new_sum + jnp.sum(
                jnp.where(allowed[None], jnp.exp(scores - shifted[:, :, None]), 0.0), axis=2
            )
            return (newest, new_sum)

        return (
            lax.cond(jnp.any(allowed), stat_update, lambda running_state: running_state, running),
            None,
        )

    stat_start = (
        jnp.full((head_count, row_count), -jnp.inf, jnp.float32),
        jnp.zeros((head_count, row_count), jnp.float32),
    )
    block_numbers = jnp.arange(block_count, dtype=jnp.int32)
    (row_max, row_sum), unused = lax.scan(stat_step, stat_start, block_numbers)
    log_norm = row_max + jnp.log(row_sum)

    def weights_of(key_block, allowed):
        scores = score_block(key_block)
        return jnp.where(allowed[None], jnp.exp(scores - log_norm[:, :, None]), 0.0)

    def output_step(running, block_index):
        allowed, key_block, value_block = block_view(block_index * key_rows, key_rows)

        def output_update(attended):
            weights_low = weights_of(key_block, allowed).astype(jnp.bfloat16)
            return attended + jnp.einsum(
                "hrk,kd->hrd", weights_low, value_block, preferred_element_type=jnp.float32
            )

        return (lax.cond(jnp.any(allowed), output_update, lambda attended: attended, running), None)

    attended, unused = lax.scan(
        output_step, jnp.zeros((head_count, row_count, head_dim), jnp.float32), block_numbers
    )
    row_delta = jnp.einsum("rhd,hrd->hr", grad_wide, attended)

    def tile_grads(key_block, value_block, allowed):
        weights = weights_of(key_block, allowed)
        weights_low = weights.astype(jnp.bfloat16)
        grad_weights = jnp.einsum(
            "rhd,kd->hrk", grad_heads, value_block, preferred_element_type=jnp.float32
        )
        grad_scores = (weights * (grad_weights - row_delta[:, :, None])).astype(jnp.bfloat16)
        return (weights_low, grad_scores)

    grad_zero = jnp.zeros((row_count, head_count, head_dim), jnp.float32)

    def joint_step(running, block_index):
        allowed, key_block, value_block = block_view(block_index * key_rows, key_rows)

        def joint_update(grad_q):
            weights_low, grad_scores = tile_grads(key_block, value_block, allowed)
            grad_k = (
                jnp.einsum(
                    "hrk,rhd->kd", grad_scores, query_heads, preferred_element_type=jnp.float32
                )
                * scaling
            )
            grad_v = jnp.einsum(
                "hrk,rhd->kd", weights_low, grad_heads, preferred_element_type=jnp.float32
            )
            grad_q = grad_q + jnp.einsum(
                "hrk,kd->rhd", grad_scores, key_block, preferred_element_type=jnp.float32
            )
            return (grad_q, grad_k, grad_v)

        def passed(grad_q):
            empty_block = jnp.zeros((key_rows, head_dim), jnp.float32)
            return (grad_q, empty_block, empty_block)

        new_grad, grad_k, grad_v = lax.cond(jnp.any(allowed), joint_update, passed, running)
        return (new_grad, (grad_k, grad_v))

    grad_q, (block_keys, block_values) = lax.scan(joint_step, grad_zero, block_numbers)
    grad_keys, grad_values = (
        lax.psum_scatter(
            block_keys.reshape(all_rows, head_dim).astype(jnp.bfloat16),
            "ctx",
            scatter_dimension=0,
            tiled=True,
        ).astype(jnp.float32),
        lax.psum_scatter(
            block_values.reshape(all_rows, head_dim).astype(jnp.bfloat16),
            "ctx",
            scatter_dimension=0,
            tiled=True,
        ).astype(jnp.float32),
    )
    grad_queries = (grad_q * scaling).astype(jnp.bfloat16).reshape(row_count, feature_width)
    return (grad_queries, grad_keys.astype(jnp.bfloat16), grad_values.astype(jnp.bfloat16))


def solution(mesh):
    return jax.shard_map(
        body,
        mesh=mesh,
        in_specs=(P("ctx", "head"), P("ctx", "head"), P("ctx", "head"), P("ctx", "head"), P(), P()),
        out_specs=(P("ctx", "head"), P("ctx", "head"), P("ctx", "head")),
        check_vma=False,
    )
```

profile of v0, /device:TPU:192, one launch (start us, length us, event | category | flops | bytes accessed | tf_op | source)
XLA Modules:
  0.0 397.3 jit_solution(4317704295099483624)
XLA Ops:
  13.7 2.1 fusion.52
  15.8 2.1 fusion.53
  17.8 2.1 fusion.54
  24.1 4.5 %compare_select_fusion.1 = s32[4096,1]{0,1:T(1,128)S(1)} fusion(s32[]{:T(128)} %bitcast.75, s32[]{:T(128)} %bitcast.76, s32[]{:T(128)} %bitcast.77, s32[]{:T(128)} %bitcast.78, s32[]{:T(128)} %bitcast.79, s32[]{:T(128)} %bitcast.81, s32[]{:T(128)} %bitcast.80), kind=kLoop, calls=%fused_computation.121 | loop fusion | flops 94208 | bytes 16412 | tf_op jit(solution)/shard_map/gather | solution.py:17
  28.5 35.9 %fusion.48 = s32[4096]{0:T(1024)S(1)} fusion(pred[4096]{0:T(1024)(128)(4,1)S(1)} %compare_reduce_fusion, pred[4096]{0:T(1024)(128)(4,1)S(1)} %compare_reduce_fusion.1, pred[4096]{0:T(1024)(128)(4,1)S(1)} %compare_reduce_fusion.2, pred[4096]{0:T(1024)(128)(4,1)S(1)} %compare_reduce_fusion.3, pred[4096]{0:T(1024)(128)(4,1)S(1)} %compare_reduce_fusion.4, ...), kind=kLoop, calls=%fused_computation.132 | loop fusion | flops 266240 | bytes 266468 | tf_op jit(solution)/shard_map/add | solution.py:17
  64.6 38.0 %while.42 = (s32[]{:T(128)}, f32[8,128]{1,0:T(8,128)S(1)}, f32[8,128]{1,0:T(8,128)S(1)}, s32[8]{0:T(128)S(1)}, s32[4096]{0:T(1024)S(1)}, /*index=5*/s32[128]{0:T...) while((s32[]{:T(128)}, f32[8,128]{1,0:T(8,128)S(1)}, ...), condition=%wide.region_8.9_spmd, body=%wide.region_2.8_spmd.sunk | while | flops 138156032 | bytes 4849441 | solution.py:70
  102.6 6.3 %all-gather.5.cloned.1.call-done = bf16[4096,128]{1,0:T(8,128)(2,1)} async-done(((bf16[128,128]{1,0:T(8,128)(2,1)}), bf16[4096,128]{1,0:T(8,128)(2,1)}) %all-gather.5.cloned.1.call-update) | async-done | bytes 1048592 | tf_op jit(solution)/shard_map/all_gather | solution.py:25
  109.0 37.9 %while.43 = (s32[]{:T(128)}, f32[8,128,128]{2,1,0:T(8,128)S(1)}, s32[8]{0:T(128)S(1)}, s32[4096]{0:T(1024)S(1)}, s32[128]{0:T(128)S(1)}, /*index=5*/s32[128]{0:T...) while((s32[]{:T(128)}, f32[8,128,128]{2,1,0:T(8,128)S(1)}, ...), condition=%wide.region_13.14_spmd, body=%wide.region_9.13_spmd.sunk | while | flops 270925824 | bytes 1716497 | solution.py:88
  111.8 2.0 conditional.7
  111.8 2.0 fusion.13
  116.5 2.0 conditional.7
  116.5 2.0 fusion.13
  121.2 2.0 conditional.7
  121.3 2.0 fusion.13
  126.0 2.0 conditional.7
  126.0 2.0 fusion.13
  130.7 2.0 conditional.7
  135.5 2.0 conditional.7
  135.5 2.0 fusion.13
  140.2 2.0 conditional.7
  144.9 2.0 conditional.7
  147.3 69.6 %while.44 = (s32[]{:T(128)}, f32[128,8,128]{2,0,1:T(8,128)S(1)}, bf16[8,512,128]{2,1,0:T(8,128)(2,1)}, bf16[8,512,128]{2,1,0:T(8,128)(2,1)}, s32[8]{0:T(128)S(1)...) while((s32[]{:T(128)}, f32[128,8,128]{2,0,1:T(8,128)S(1)}, ...), condition=%wide.region_18.19_spmd, body=%wide.region_14.18_spmd.sunk | while | flops 675282944 | bytes 12862293 | solution.py:130
  150.0 5.2 %conditional.8 = (f32[128,8,128]{2,0,1:T(8,128)S(1)}, bf16[1,512,128]{2,1,0:T(8,128)(2,1)S(1)}, bf16[1,512,128]{2,1,0:T(8,128)(2,1)S(1)}) conditional(s32[]{:T(128)} %convert_element_type.66, f32[128,8,128]{2,0,1:T(8,128)S(1)} %get-tuple-element.916, (pred[128,512]{0,1:T(8,128)(4,1)S(1)}, bf16[4096,128]{1,0:T(8,128)(2,1)}, s32[]{:T(128)}, ...), branch_computations={%region_16.16_spmd, %region_17.17_spmd} | conditional | flops 675020800 | bytes 12264984 | solution.py:127
  158.7 5.2 %conditional.8 = (f32[128,8,128]{2,0,1:T(8,128)S(1)}, bf16[1,512,128]{2,1,0:T(8,128)(2,1)S(1)}, bf16[1,512,128]{2,1,0:T(8,128)(2,1)S(1)}) conditional(s32[]{:T(128)} %convert_element_type.66, f32[128,8,128]{2,0,1:T(8,128)S(1)} %get-tuple-element.916, (pred[128,512]{0,1:T(8,128)(4,1)S(1)}, bf16[4096,128]{1,0:T(8,128)(2,1)}, s32[]{:T(128)}, ...), branch_computations={%region_16.16_spmd, %region_17.17_spmd} | conditional | flops 675020800 | bytes 12264984 | solution.py:127
  167.4 5.2 %conditional.8 = (f32[128,8,128]{2,0,1:T(8,128)S(1)}, bf16[1,512,128]{2,1,0:T(8,128)(2,1)S(1)}, bf16[1,512,128]{2,1,0:T(8,128)(2,1)S(1)}) conditional(s32[]{:T(128)} %convert_element_type.66, f32[128,8,128]{2,0,1:T(8,128)S(1)} %get-tuple-element.916, (pred[128,512]{0,1:T(8,128)(4,1)S(1)}, bf16[4096,128]{1,0:T(8,128)(2,1)}, s32[]{:T(128)}, ...), branch_computations={%region_16.16_spmd, %region_17.17_spmd} | conditional | flops 675020800 | bytes 12264984 | solution.py:127
  176.1 5.2 %conditional.8 = (f32[128,8,128]{2,0,1:T(8,128)S(1)}, bf16[1,512,128]{2,1,0:T(8,128)(2,1)S(1)}, bf16[1,512,128]{2,1,0:T(8,128)(2,1)S(1)}) conditional(s32[]{:T(128)} %convert_element_type.66, f32[128,8,128]{2,0,1:T(8,128)S(1)} %get-tuple-element.916, (pred[128,512]{0,1:T(8,128)(4,1)S(1)}, bf16[4096,128]{1,0:T(8,128)(2,1)}, s32[]{:T(128)}, ...), branch_computations={%region_16.16_spmd, %region_17.17_spmd} | conditional | flops 675020800 | bytes 12264984 | solution.py:127
  184.8 5.2 %conditional.8 = (f32[128,8,128]{2,0,1:T(8,128)S(1)}, bf16[1,512,128]{2,1,0:T(8,128)(2,1)S(1)}, bf16[1,512,128]{2,1,0:T(8,128)(2,1)S(1)}) conditional(s32[]{:T(128)} %convert_element_type.66, f32[128,8,128]{2,0,1:T(8,128)S(1)} %get-tuple-element.916, (pred[128,512]{0,1:T(8,128)(4,1)S(1)}, bf16[4096,128]{1,0:T(8,128)(2,1)}, s32[]{:T(128)}, ...), branch_computations={%region_16.16_spmd, %region_17.17_spmd} | conditional | flops 675020800 | bytes 12264984 | solution.py:127
  193.5 5.2 %conditional.8 = (f32[128,8,128]{2,0,1:T(8,128)S(1)}, bf16[1,512,128]{2,1,0:T(8,128)(2,1)S(1)}, bf16[1,512,128]{2,1,0:T(8,128)(2,1)S(1)}) conditional(s32[]{:T(128)} %convert_element_type.66, f32[128,8,128]{2,0,1:T(8,128)S(1)} %get-tuple-element.916, (pred[128,512]{0,1:T(8,128)(4,1)S(1)}, bf16[4096,128]{1,0:T(8,128)(2,1)}, s32[]{:T(128)}, ...), branch_computations={%region_16.16_spmd, %region_17.17_spmd} | conditional | flops 675020800 | bytes 12264984 | solution.py:127
  202.2 5.2 %conditional.8 = (f32[128,8,128]{2,0,1:T(8,128)S(1)}, bf16[1,512,128]{2,1,0:T(8,128)(2,1)S(1)}, bf16[1,512,128]{2,1,0:T(8,128)(2,1)S(1)}) conditional(s32[]{:T(128)} %convert_element_type.66, f32[128,8,128]{2,0,1:T(8,128)S(1)} %get-tuple-element.916, (pred[128,512]{0,1:T(8,128)(4,1)S(1)}, bf16[4096,128]{1,0:T(8,128)(2,1)}, s32[]{:T(128)}, ...), branch_computations={%region_16.16_spmd, %region_17.17_spmd} | conditional | flops 675020800 | bytes 12264984 | solution.py:127
  210.9 5.2 %conditional.8 = (f32[128,8,128]{2,0,1:T(8,128)S(1)}, bf16[1,512,128]{2,1,0:T(8,128)(2,1)S(1)}, bf16[1,512,128]{2,1,0:T(8,128)(2,1)S(1)}) conditional(s32[]{:T(128)} %convert_element_type.66, f32[128,8,128]{2,0,1:T(8,128)S(1)} %get-tuple-element.916, (pred[128,512]{0,1:T(8,128)(4,1)S(1)}, bf16[4096,128]{1,0:T(8,128)(2,1)}, s32[]{:T(128)}, ...), branch_computations={%region_16.16_spmd, %region_17.17_spmd} | conditional | flops 675020800 | bytes 12264984 | solution.py:127
  218.2 83.3 %reduce-scatter.5.cloned.1.call-done = bf16[128,128]{1,0:T(8,128)(2,1)} async-done(((bf16[4096,128]{1,0:T(8,128)(2,1)}), bf16[128,128]{1,0:T(8,128)(2,1)}) %reduce-scatter.5.cloned.1.call-update) | async-done | bytes 32784 | tf_op jit(solution)/shard_map/reduce_scatter | solution.py:138
  301.5 89.2 %reduce-scatter.3.cloned.1.call-done = bf16[128,128]{1,0:T(8,128)(2,1)} async-done(((bf16[4096,128]{1,0:T(8,128)(2,1)}), bf16[128,128]{1,0:T(8,128)(2,1)}) %reduce-scatter.3.cloned.1.call-update) | async-done | bytes 32784 | tf_op jit(solution)/shard_map/reduce_scatter | solution.py:132
  (259 shorter events, 130.4 us)
Async XLA Ops:
  7.2 57.4 %all-gather.3.cloned.1.call-start = ((), (), s32[]{:S(2)}) async-start(), calls=%async_computation.2 | async-start | bytes 1081344 | tf_op jit(solution)/shard_map/all_gather | solution.py:24
  7.9 101.1 %all-gather.5.cloned.1.call-start = ((), (), s32[]{:S(2)}) async-start(), calls=%async_computation.3 | async-start | bytes 1081344 | tf_op jit(solution)/shard_map/all_gather | solution.py:25
  8.6 292.8 %reduce-scatter.5.cloned.1.call-start = ((), (), s32[]{:S(2)}) async-start(), calls=%async_computation.5 | async-start | bytes 1081344 | tf_op jit(solution)/shard_map/reduce_scatter | solution.py:138
  216.9 173.9 %reduce-scatter.3.cloned.1.call-start = ((), (), s32[]{:S(2)}) async-start(), calls=%async_computation.4 | async-start | bytes 1081344 | tf_op jit(solution)/shard_map/reduce_scatter | solution.py:132
Sparse Core Ops, SparseCore 0:
  10.6 48.5 all-gather.2
  61.7 47.2 all-gather.4
  217.0 84.4 reduce-scatter.4
  306.2 84.5 reduce-scatter.2
where the time goes:
time: 401 us; the launch traced here: 397 us
  waiting for transfers between devices  181 us (45%)
  other arithmetic  69 us (17%)
  matrix products  68.1 us (17%)
  local copies, waits for them, and re-layouts  32.7 us (8%)
  loops' own time  32.6 us (8%)
  between operations  14 us (3%)
    reduce_scatter x1, waiting for transfers between devices, body(): lax.psum_scatter(block_keys.reshape(all_rows, head_dim).astype(jnp.bfloat...  89.2 us
    reduce_scatter x1, waiting for transfers between devices, body(): lax.psum_scatter(block_values.reshape(all_rows, head_dim).astype(jnp.bflo...  83.3 us
    add x1, other arithmetic, body(): stretch_order[row_index // stretch_rows] * stretch_rows  35.9 us
    dot_general x16, matrix products, score_block(): jnp.einsum('rhd,kd->hrk', query_heads, key_block, preferred_element_type=...  22.9 us
    and x24, other arithmetic, block_view(): (key_pos[None, :] <= my_pos[:, None]) & (key_pos[None, :] >= my_first[:,...  19.2 us
    dot_general x8, matrix products, output_update(): jnp.einsum('hrk,kd->hrd', weights_low, value_block, preferred_element_typ...  15.8 us
    dynamic_slice x24, local copies, waits for them, and re-layouts, body(): (row_max, row_sum), unused = lax.scan(stat_step, stat_start, block_numbers)  14.3 us
    dot_general x8, matrix products, joint_update(): jnp.einsum('hrk,kd->rhd', grad_scores, key_block, preferred_element_type=...  11.6 us
  transfers between devices with their start and end apart: 4, of which 3 were waited for; matrix products, arithmetic and copies ran while one was open for 21% of the time, Pallas kernels for 0%

commit v1 on v0

v1 whole, which is shorter than its diff:
```python
import functools

import jax
import jax.numpy as jnp
from jax import lax
from jax.experimental import pallas as pl
from jax.experimental.pallas import tpu as pltpu
from jax.sharding import PartitionSpec as P

MESH = pl.DeviceIdType.MESH
F32, BF16 = jnp.float32, jnp.bfloat16
RING = 4
HEADS, DIM = 8, 128
STRETCH = 64
STRETCHES = 64
COLS = HEADS * STRETCH
WIN = 34
WROWS = WIN * STRETCH
KC = 1088
NEG = -1e30
N_AG = 64
N_RS = 32


def dot_nt(a, b):
    return lax.dot_general(a, b, (((1,), (1,)), ((), ())), preferred_element_type=F32)


def dot_nn(a, b):
    return lax.dot_general(a, b, (((1,), (0,)), ((), ())), preferred_element_type=F32)


def fold8(v, op):
    parts = v.reshape(v.shape[0] // 8, 8, v.shape[1])
    return op(parts, axis=0)


def kernel(
    q_hbm, k_hbm, v_hbm, g_hbm, len_ref, ord_ref, inv_ref,
    dq_ref, dk_ref, dv_ref,
    gkv, q_in, g_in, q_s, g_s, qn_s, gn_s, ksw, vsw, ktw, sbuf, pbuf, dsbuf, dkw, dvw,
    part_a, part_b, pair_a, pair_b, s0_a, s0_b, r1_a, r1_b, s1_a, s1_b, r2_a, r2_b,
    loc_sem, ag_send, ag_recv, rs_send, rs_recv,
):
    me = lax.axis_index("ctx")
    head = lax.axis_index("head")
    c = lax.rem(me, 2)
    x = lax.rem(lax.div(me, 2), RING)
    y = lax.div(me, 2 * RING)
    oc = 1 - c

    def wrap(v):
        return lax.rem(v + RING, RING)

    x1, x2, x3 = wrap(x + 1), wrap(x + 2), wrap(x + 3)
    y1, y2, y3 = wrap(y + 1), wrap(y + 2), wrap(y + 3)

    def dev(yy, xx, cc):
        return ((yy * RING + xx) * 2 + cc, head)

    right, left = dev(y, x1, c), dev(y, x3, c)
    up, down = dev(y1, x, c), dev(y3, x, c)
    sib = dev(y, x, oc)

    loads = [
        pltpu.make_async_copy(q_hbm, q_in, loc_sem.at[0]),
        pltpu.make_async_copy(g_hbm, g_in, loc_sem.at[1]),
    ]
    own = []
    for h in range(2):
        rows = pl.ds(h * STRETCH, STRETCH)
        own.append(pltpu.make_async_copy(k_hbm.at[rows], gkv.at[2 * me + h, 0], loc_sem.at[2 + 2 * h]))
        own.append(pltpu.make_async_copy(v_hbm.at[rows], gkv.at[2 * me + h, 1], loc_sem.at[3 + 2 * h]))
    for cp in own + loads:
        cp.start()

    barrier = pltpu.get_barrier_semaphore()
    for peer in (right, left, up, down, sib):
        pl.semaphore_signal(barrier, inc=1, device_id=peer, device_id_type=MESH)
    pl.semaphore_wait(barrier, 5)
    for cp in own:
        cp.wait()

    sent = []
    state = {"n": 0}

    def new_slot():
        state["n"] += 1
        return state["n"] - 1

    def send(ref, k, to):
        cp = pltpu.make_async_remote_copy(
            src_ref=ref, dst_ref=ref, send_sem=ag_send.at[k], recv_sem=ag_recv.at[k],
            device_id=to, device_id_type=MESH,
        )
        cp.start()
        sent.append(cp)

    def arrive(ref, k):
        pltpu.make_async_remote_copy(
            src_ref=ref, dst_ref=ref, send_sem=ag_send.at[k], recv_sem=ag_recv.at[k],
            device_id=sib, device_id_type=MESH,
        ).wait_recv()

    def first_block(yy, xx, cc):
        return ((yy * RING + xx) * 2 + cc) * 2

    def node(yy, xx, cc=None):
        return gkv.at[pl.ds(first_block(yy, xx, c if cc is None else cc), 2)]

    def sides_of(yy, xx, side):
        return gkv.at[pl.ds(first_block(yy, xx, c), 2), side]

    def half_of(yy, xx, cc, half):
        return gkv.at[first_block(yy, xx, cc) + half]

    def quarter(yy, xx, half, side):
        return gkv.at[first_block(yy, xx, c) + half, side]

    sib_waits = []

    def to_sib(cut):
        k = new_slot()
        send(cut(c), k, sib)
        sib_waits.append((cut(oc), k))

    mine = node(y, x)
    k_r, k_l, k_u, k_d = new_slot(), new_slot(), new_slot(), new_slot()
    send(mine, k_r, right)
    send(mine, k_l, left)
    send(mine, k_u, up)
    send(mine, k_d, down)
    to_sib(lambda cc: node(y, x, cc))

    lo, hi = 0, 1
    far = {}
    second = []

    def first_hop(k, yy, xx, along, opposite, side, half, sides, tag):
        arrive(node(yy, xx), k)
        kf = new_slot()
        send(sides_of(yy, xx, side), kf, opposite)
        far[tag] = kf
        ks_ = []
        for to in sides:
            kk = new_slot()
            send(half_of(yy, xx, c, half), kk, to)
            ks_.append(kk)
        to_sib(lambda cc: node(yy, xx, cc))
        return ks_

    def opp_slots(names):
        return names

    from_l = first_hop(k_r, y, x3, None, right, lo, 0, (up, down), "xl")
    from_r = first_hop(k_l, y, x1, None, left, hi, 0, (up, down), "xr")
    from_d = first_hop(k_u, y3, x, None, up, lo, 1, (right, left), "yd")
    from_u = first_hop(k_d, y1, x, None, down, hi, 1, (right, left), "yu")

    arrive(sides_of(y, x2, lo), far["xl"])
    arrive(sides_of(y, x2, hi), far["xr"])
    xf = []
    for to in (up, down):
        kk = new_slot()
        send(half_of(y, x2, c, 0), kk, to)
        xf.append(kk)
    to_sib(lambda cc: node(y, x2, cc))
    arrive(sides_of(y2, x, lo), far["yd"])
    arrive(sides_of(y2, x, hi), far["yu"])
    yf = []
    for to in (right, left):
        kk = new_slot()
        send(half_of(y2, x, c, 1), kk, to)
        yf.append(kk)
    to_sib(lambda cc: node(y2, x, cc))

    last = []

    def second_hop(k, yy, xx, half, side, to, fy, fx):
        arrive(half_of(yy, xx, c, half), k)
        kk = new_slot()
        send(quarter(yy, xx, half, side), kk, to)
        to_sib(lambda cc: half_of(yy, xx, cc, half))
        return kk

    for xx, slots in ((x3, from_l), (x1, from_r), (x2, xf)):
        ka = second_hop(slots[0], y3, xx, 0, lo, up, y2, xx)
        kb = second_hop(slots[1], y1, xx, 0, hi, down, y2, xx)
        last.append((y2, xx, 0, ka, kb))
    for yy, slots in ((y3, from_d), (y1, from_u), (y2, yf)):
        ka = second_hop(slots[0], yy, x3, 1, lo, right, yy, x2)
        kb = second_hop(slots[1], yy, x1, 1, hi, left, yy, x2)
        last.append((yy, x2, 1, ka, kb))
    for yy, xx, half, ka, kb in last:
        arrive(quarter(yy, xx, half, lo), ka)
        arrive(quarter(yy, xx, half, hi), kb)
        to_sib(lambda cc, yy=yy, xx=xx, half=half: half_of(yy, xx, cc, half))

    for cp in loads:
        cp.wait()
    for a in range(2):
        for h in range(HEADS):
            src = (pl.ds(a * STRETCH, STRETCH), pl.ds(h * DIM, DIM))
            q_s[a, pl.ds(h * STRETCH, STRETCH), :] = q_in[src]
            g_s[a, pl.ds(h * STRETCH, STRETCH), :] = g_in[src]

    for ref, k in sib_waits:
        arrive(ref, k)

    spots, base = [], []
    for a in range(2):
        p = ord_ref[2 * me + a]
        spots.append(p)
        base.append(jnp.maximum(lax.div(p, 2) * 2 - 32, 0))

    def window_step(w, carry):
        rows = pl.ds(pl.multiple_of(w * STRETCH, STRETCH), STRETCH)
        for a in range(2):
            b = inv_ref[base[a] + w]
            ksw[a, rows, :] = gkv[b, 0]
            vsw[a, rows, :] = gkv[b, 1]
        return carry

    lax.fori_loop(0, WIN, window_step, 0)

    def turn_step(j, carry):
        rows = pl.ds(pl.multiple_of(j * 128, 128), 128)
        for a in range(2):
            ktw[a, :, rows] = ksw[a, rows, :].T
        return carry

    lax.fori_loop(0, WIN // 2, turn_step, 0)

    scale = DIM ** -0.5
    log2e = 1.4426950408889634
    starts = [jnp.int32(0)]
    for d in range(3):
        starts.append(starts[-1] + len_ref[d])
    lane = lax.broadcasted_iota(jnp.int32, (1, 128), 1)
    row_in = jnp.where(lane >= STRETCH, lane - STRETCH, lane)
    pos_row, first_row = [], []
    for a in range(2):
        pr = spots[a] * STRETCH + row_in
        fr = jnp.zeros_like(pr)
        for st in starts:
            fr = jnp.maximum(fr, jnp.where(st <= pr, st, 0))
        pos_row.append(pr)
        first_row.append(fr)

    groups = COLS // 128

    def score_step(j, carry):
        new = []
        for a in range(2):
            s = dot_nt(ksw[a, pl.ds(pl.multiple_of(j * KC, 16), KC), :], q_s[a])
            first_key = base[a] * STRETCH + j * KC
            kpos = first_key + lax.broadcasted_iota(jnp.int32, (KC, 128), 0)
            ok = (kpos <= pos_row[a]) & (kpos >= first_row[a])
            for g in range(groups):
                cols = pl.ds(g * 128, 128)
                sg = jnp.where(ok, s[:, g * 128:(g + 1) * 128] * (scale * log2e), NEG)
                sbuf[a, pl.ds(pl.multiple_of(j * KC, 8), KC), cols] = sg
                new.append(jnp.maximum(carry[a * groups + g], fold8(sg, jnp.max)))
        return tuple(new)

    tops = lax.fori_loop(
        0, WROWS // KC, score_step, tuple(jnp.full((8, 128), NEG, F32) for _ in range(2 * groups))
    )
    tops = [jnp.max(t, axis=0, keepdims=True) for t in tops]

    def weight_step(j, carry):
        new = []
        rows = pl.ds(pl.multiple_of(j * KC, 16), KC)
        for a in range(2):
            dp = dot_nt(vsw[a, rows, :], g_s[a])
            for g in range(groups):
                cols = pl.ds(g * 128, 128)
                pw = jnp.exp2(sbuf[a, rows, cols] - tops[a * groups + g])
                dpg = dp[:, g * 128:(g + 1) * 128]
                pbuf[a, rows, cols] = pw.astype(BF16)
                sbuf[a, rows, cols] = dpg
                total, dsum = carry[a * groups + g]
                new.append((total + fold8(pw, jnp.sum), dsum + fold8(pw * dpg, jnp.sum)))
        return tuple(new)

    zero = jnp.zeros((8, 128), F32)
    sums = lax.fori_loop(
        0, WROWS // KC, weight_step, tuple((zero, zero) for _ in range(2 * groups))
    )
    inv_l, delta = [], []
    for total, dsum in sums:
        r = 1.0 / jnp.sum(total, axis=0, keepdims=True)
        inv_l.append(r)
        delta.append(jnp.sum(dsum, axis=0, keepdims=True) * r)

    for a in range(2):
        for g in range(groups):
            rows = pl.ds(g * 128, 128)
            col = jnp.broadcast_to(inv_l[a * groups + g], (128, 128)).T
            qn_s[a, rows, :] = (q_s[a, rows, :].astype(F32) * (col * scale)).astype(BF16)
            gn_s[a, rows, :] = (g_s[a, rows, :].astype(F32) * col).astype(BF16)

    def grad_step(j, carry):
        rows = pl.ds(pl.multiple_of(j * KC, 16), KC)
        for a in range(2):
            for g in range(groups):
                cols = pl.ds(g * 128, 128)
                pw = pbuf[a, rows, cols].astype(F32)
                dsbuf[a, rows, cols] = (pw * (sbuf[a, rows, cols] - delta[a * groups + g])).astype(BF16)
            spans = pl.ds(j * (KC // STRETCH), KC // STRETCH)
            wide = (KC // STRETCH, STRETCH, DIM)
            dvw[a, spans] = dot_nn(pbuf[a, rows, :], gn_s[a]).reshape(wide)
            dkw[a, spans] = dot_nn(dsbuf[a, rows, :], qn_s[a]).reshape(wide)
        return carry

    lax.fori_loop(0, WROWS // KC, grad_step, 0)
    for a in range(2):
        dkw[a, WIN] = jnp.zeros((STRETCH, DIM), F32)
        dvw[a, WIN] = jnp.zeros((STRETCH, DIM), F32)

    def unsort(cc, i):
        yy, xx = lax.div(i, RING), lax.rem(i, RING)
        for half, out in ((0, part_a.at[cc, xx]), (1, part_b.at[cc, yy])):
            s = ord_ref[2 * (2 * i + cc) + half]
            at = []
            for a in range(2):
                off = s - base[a]
                at.append(jnp.where((off >= 0) & (off < WIN), off, WIN))
            for kv, w in ((0, dkw), (1, dvw)):
                both = w[0, at[0]] + w[1, at[1]]
                other = yy if half == 0 else xx
                out[kv, other] = both.astype(BF16)

    def rs_copy(src, dst, k, to):
        return pltpu.make_async_remote_copy(
            src_ref=src, dst_ref=dst, send_sem=rs_send.at[k], recv_sem=rs_recv.at[k],
            device_id=to, device_id_type=MESH,
        )

    lax.fori_loop(0, RING * RING, lambda i, z: (unsort(oc, i), z)[1], 0)
    swap_a = rs_copy(part_a.at[oc], pair_a, 0, sib)
    swap_b = rs_copy(part_b.at[oc], pair_b, 1, sib)
    swap_a.start()
    swap_b.start()
    lax.fori_loop(0, RING * RING, lambda i, z: (unsort(c, i), z)[1], 0)

    swap_a.wait()
    swap_b.wait()

    def pair_step(i, carry):
        for part, pair, out in ((part_a, pair_a, s0_a), (part_b, pair_b, s0_b)):
            for kv in range(2):
                out[i, kv] = (part[c, i, kv].astype(F32) + pair[i, kv].astype(F32)).astype(BF16)
        return carry

    lax.fori_loop(0, RING, pair_step, 0)

    def ring_start(buf, recv, k0, p1, p2, p3, fwd, bwd):
        cps = [
            rs_copy(buf.at[p2, 0], recv.at[0], k0, fwd),
            rs_copy(buf.at[p2, 1], recv.at[1], k0 + 1, bwd),
            rs_copy(buf.at[p1, 1], recv.at[2], k0 + 2, fwd),
            rs_copy(buf.at[p3, 0], recv.at[3], k0 + 3, bwd),
        ]
        for cp in cps:
            cp.start()
        return cps

    def ring_mid(buf, recv, k0, p1, p2, p3, fwd, bwd, cps):
        cps[0].wait_recv()
        buf[p1, 0] = (buf[p1, 0].astype(F32) + recv[0].astype(F32)).astype(BF16)
        cp = rs_copy(buf.at[p1, 0], recv.at[4], k0 + 4, fwd)
        cp.start()
        cps.append(cp)
        cps[1].wait_recv()
        buf[p3, 1] = (buf[p3, 1].astype(F32) + recv[1].astype(F32)).astype(BF16)
        cp = rs_copy(buf.at[p3, 1], recv.at[5], k0 + 5, bwd)
        cp.start()
        cps.append(cp)

    def ring_end(buf, recv, at, cps):
        for i in range(2, 6):
            cps[i].wait_recv()
        k_sum = buf[at, 0].astype(F32) + recv[3].astype(F32) + recv[4].astype(F32)
        v_sum = buf[at, 1].astype(F32) + recv[2].astype(F32) + recv[5].astype(F32)
        return k_sum.astype(BF16), v_sum.astype(BF16)

    xs, ys = (x1, x2, x3, right, left), (y1, y2, y3, up, down)
    ca = ring_start(s0_a, r1_a, 2, *xs)
    cb = ring_start(s0_b, r1_b, 8, *ys)

    for a in range(2):
        dqt = dot_nn(ktw[a], dsbuf[a])
        for g in range(groups):
            block = (dqt[:, g * 128:(g + 1) * 128] * (inv_l[a * groups + g] * scale)).T.astype(BF16)
            for i in range(2):
                dq_ref[pl.ds(a * STRETCH, STRETCH), pl.ds((2 * g + i) * DIM, DIM)] = block[i * STRETCH:(i + 1) * STRETCH]

    ring_mid(s0_a, r1_a, 2, *xs, ca)
    ring_mid(s0_b, r1_b, 8, *ys, cb)
    k_sum, v_sum = ring_end(s0_a, r1_a, x, ca)
    for i in range(RING):
        s1_a[i, 0] = k_sum[i]
        s1_a[i, 1] = v_sum[i]
    ca2 = ring_start(s1_a, r2_a, 14, *ys)
    k_sum, v_sum = ring_end(s0_b, r1_b, y, cb)
    for i in range(RING):
        s1_b[i, 0] = k_sum[i]
        s1_b[i, 1] = v_sum[i]
    cb2 = ring_start(s1_b, r2_b, 20, *xs)
    ring_mid(s1_a, r2_a, 14, *ys, ca2)
    ring_mid(s1_b, r2_b, 20, *xs, cb2)
    k_sum, v_sum = ring_end(s1_a, r2_a, y, ca2)
    dk_ref[pl.ds(0, STRETCH), :] = k_sum
    dv_ref[pl.ds(0, STRETCH), :] = v_sum
    k_sum, v_sum = ring_end(s1_b, r2_b, x, cb2)
    dk_ref[pl.ds(STRETCH, STRETCH), :] = k_sum
    dv_ref[pl.ds(STRETCH, STRETCH), :] = v_sum

    for cp in sent + ca + cb + ca2 + cb2:
        cp.wait_send()


def body(queries, keys, values, grad_out, doc_lengths, stretch_order):
    slots = jnp.arange(STRETCHES, dtype=jnp.int32)
    inverse = jnp.sum(
        jnp.where(stretch_order[None, :] == slots[:, None], slots[None, :], 0), axis=1, dtype=jnp.int32
    )
    anyspec = pl.BlockSpec(memory_space=pl.ANY)
    smem = pl.BlockSpec(memory_space=pltpu.SMEM)
    vmem = pl.BlockSpec(memory_space=pltpu.VMEM)
    half = (STRETCH, DIM)
    return pl.pallas_call(
        kernel,
        out_shape=(
            jax.ShapeDtypeStruct(queries.shape, BF16),
            jax.ShapeDtypeStruct(keys.shape, BF16),
            jax.ShapeDtypeStruct(values.shape, BF16),
        ),
        in_specs=[anyspec] * 4 + [smem] * 3,
        out_specs=(vmem, vmem, vmem),
        scratch_shapes=[
            pltpu.VMEM((STRETCHES, 2) + half, BF16),
            pltpu.VMEM((2 * STRETCH, HEADS * DIM), BF16),
            pltpu.VMEM((2 * STRETCH, HEADS * DIM), BF16),
            pltpu.VMEM((2, COLS, DIM), BF16),
            pltpu.VMEM((2, COLS, DIM), BF16),
            pltpu.VMEM((2, COLS, DIM), BF16),
            pltpu.VMEM((2, COLS, DIM), BF16),
            pltpu.VMEM((2, WROWS, DIM), BF16),
            pltpu.VMEM((2, WROWS, DIM), BF16),
            pltpu.VMEM((2, DIM, WROWS), BF16),
            pltpu.VMEM((2, WROWS, COLS), F32),
            pltpu.VMEM((2, WROWS, COLS), BF16),
            pltpu.VMEM((2, WROWS, COLS), BF16),
            pltpu.VMEM((2, WIN + 1) + half, F32),
            pltpu.VMEM((2, WIN + 1) + half, F32),
            pltpu.VMEM((2, RING, 2, RING) + half, BF16),
            pltpu.VMEM((2, RING, 2, RING) + half, BF16),
            pltpu.VMEM((RING, 2, RING) + half, BF16),
            pltpu.VMEM((RING, 2, RING) + half, BF16),
            pltpu.VMEM((RING, 2, RING) + half, BF16),
            pltpu.VMEM((RING, 2, RING) + half, BF16),
            pltpu.VMEM((6, RING) + half, BF16),
            pltpu.VMEM((6, RING) + half, BF16),
            pltpu.VMEM((RING, 2) + half, BF16),
            pltpu.VMEM((RING, 2) + half, BF16),
            pltpu.VMEM((6,) + half, BF16),
            pltpu.VMEM((6,) + half, BF16),
            pltpu.SemaphoreType.DMA((6,)),
            pltpu.SemaphoreType.DMA((N_AG,)),
            pltpu.SemaphoreType.DMA((N_AG,)),
            pltpu.SemaphoreType.DMA((N_RS,)),
            pltpu.SemaphoreType.DMA((N_RS,)),
        ],
        compiler_params=pltpu.CompilerParams(
            collective_id=0, has_side_effects=True, vmem_limit_bytes=56 * 1024 * 1024
        ),
    )(queries, keys, values, grad_out, doc_lengths, stretch_order, inverse)


def solution(mesh):
    return jax.shard_map(
        body,
        mesh=mesh,
        in_specs=(P("ctx", "head"), P("ctx", "head"), P("ctx", "head"), P("ctx", "head"), P(), P()),
        out_specs=(P("ctx", "head"), P("ctx", "head"), P("ctx", "head")),
        check_vma=False,
    )
```

time: 401 us -> 54.7 us (0.14)
  waiting for transfers between devices: 181 us -> 0 us
  matrix products: 68.1 us -> 0 us
  other arithmetic: 69 us -> 1.28 us
  Pallas kernels: 0 us -> 49.5 us
  loops' own time: 32.6 us -> 0 us
  local copies, waits for them, and re-layouts: 32.7 us -> 3.06 us
  between operations: 14 us -> 0.65 us
    reduce_scatter x2 -> x0, waiting for transfers between devices: 173 us -> none  [the longest x1 89.2 us: body(): lax.psum_scatter(block_keys.reshape(all_rows, head_dim).astype(jnp.bfloat...]
    dot_general x56 -> x0, matrix products: 68.1 us -> none  [the longest x16 22.9 us: score_block(): jnp.einsum('rhd,kd->hrk', query_heads, key_block, preferred_element_type=...]
    pallas_call x0 -> x1, Pallas kernels: none -> 49.5 us  [body(): pl.pallas_call(kernel, out_shape=(jax.ShapeDtypeStruct(queries.shape, BF1...]
    add x10 -> x0, other arithmetic: 36 us -> none  [the longest x1 35.9 us: body(): stretch_order[row_index // stretch_rows] * stretch_rows]
    another operation x27 -> x0, loops' own time: 32.6 us -> none  [the longest x1 10.7 us: body(): (row_max, row_sum), unused = lax.scan(stat_step, stat_start, block_numbers)]
    and x24 -> x0, other arithmetic: 19.2 us -> none  [block_view(): (key_pos[None, :] <= my_pos[:, None]) & (key_pos[None, :] >= my_first[:,...]
    dynamic_slice x49 -> x0, local copies, waits for them, and re-layouts: 16.2 us -> none  [the longest x24 14.3 us: body(): (row_max, row_sum), unused = lax.scan(stat_step, stat_start, block_numbers)]
    gather x58 -> x0, other arithmetic: 7.86 us -> none  [body(): stretch_order[row_index // stretch_rows] * stretch_rows]
  transfers between devices with their start and end apart: 4 -> 0, of which waited for: 3 -> 0; matrix products, arithmetic and copies ran while one was open for 21% -> 0% of each run, Pallas kernels for 0% -> 0%
where the time goes in v1:
time: 54.7 us; the launch traced here: 54.5 us
  Pallas kernels  49.5 us (90%)
  local copies, waits for them, and re-layouts  3.06 us (6%)
  other arithmetic  1.28 us (2%)
  between operations  0.65 us (1%)
    pallas_call x1, Pallas kernels, body(): pl.pallas_call(kernel, out_shape=(jax.ShapeDtypeStruct(queries.shape, BF1...  49.5 us
    unnamed x7, local copies, waits for them, and re-layouts  3.06 us
    reduce_sum x1, other arithmetic, body(): jnp.sum(jnp.where(stretch_order[None, :] == slots[:, None], slots[None, :...  1.28 us

profile of v1, /device:TPU:192, one launch (start us, length us, event | category | flops | bytes accessed | tf_op | source)
XLA Modules:
  0.0 54.5 jit_solution(12499034382926175148)
XLA Ops:
  0.6 1.3 %select_reduce_fusion.inv_ref = s32[64]{0:T(128)} fusion(s32[64]{0:T(128)} %ord_ref.1), kind=kLoop, calls=%fused_computation | loop fusion | flops 12224 | bytes 512 | tf_op jit(solution)/shard_map/reduce_sum | solution.py:426
  1.9 49.5 %shard_map.85 = (bf16[128,1024]{1,0:T(8,128)(2,1)}, bf16[128,128]{1,0:T(8,128)(2,1)}, bf16[128,128]{1,0:T(8,128)(2,1)}) custom-call(bf16[128,1024]{1,0:T(8,128)(2,1)} %q_hbm.1, bf16[128,128]{1,0:T(8,128)(2,1)} %k_hbm.1, bf16[128,128]{1,0:T(8,128)(2,1)} %v_hbm.1, bf16[128,1024]{1,0:T(8,128)(2,1)} %g_hbm.1, s32[4]{0:T(128)} %len_ref.1, s32[64]{0:T(128)} %ord_ref.1, ...), custom_call_target="tpu_custom_call" | custom-call | tf_op jit(solution)/shard_map/pallas_call | solution.py:433
  51.4 0.0 copy-start.1
  51.4 1.7 %copy.12 = bf16[128,1024]{1,0:T(8,128)(2,1)} copy(bf16[128,1024]{1,0:T(8,128)(2,1)} %get-tuple-element.6) | data formatting | bytes 524288
  53.1 0.0 copy-done.1
  53.1 0.0 copy-start
  53.1 0.6 %copy.13 = bf16[128,128]{1,0:T(8,128)(2,1)} copy(bf16[128,128]{1,0:T(8,128)(2,1)S(1)} %copy-done.1) | data formatting | bytes 65536
  53.7 0.2 copy-done
  53.9 0.6 %copy.14 = bf16[128,128]{1,0:T(8,128)(2,1)} copy(bf16[128,128]{1,0:T(8,128)(2,1)S(1)} %copy-done) | data formatting | bytes 65536
Async XLA Ops:
  51.4 1.7 %copy-start.1 = (bf16[128,128]{1,0:T(8,128)(2,1)S(1)}, bf16[128,128]{1,0:T(8,128)(2,1)}, u32[]{:S(2)}) copy-start(bf16[128,128]{1,0:T(8,128)(2,1)} %get-tuple-element.7) | copy-start | bytes 98308
  53.1 0.8 %copy-start = (bf16[128,128]{1,0:T(8,128)(2,1)S(1)}, bf16[128,128]{1,0:T(8,128)(2,1)}, u32[]{:S(2)}) copy-start(bf16[128,128]{1,0:T(8,128)(2,1)} %get-tuple-element.8) | copy-start | bytes 98308

commit v2 on v0

v2 whole, which is shorter than its diff:
```python
import functools

import jax
import jax.numpy as jnp
from jax import lax
from jax.experimental import pallas as pl
from jax.experimental.pallas import tpu as pltpu
from jax.sharding import PartitionSpec as P

MESH = pl.DeviceIdType.MESH
F32, BF16 = jnp.float32, jnp.bfloat16
RING = 4
CHIPS = RING * RING
HEADS, DIM = 8, 128
STRETCH = 64
STRETCHES = 64
COLS = HEADS * STRETCH
GROUPS = COLS // 128
WIN = 34
WROWS = WIN * STRETCH
KC = 1088
NEG = -1e30
N_AG = 128
N_RS = 48


def dot_nt(a, b):
    return lax.dot_general(a, b, (((1,), (1,)), ((), ())), preferred_element_type=F32)


def dot_nn(a, b):
    return lax.dot_general(a, b, (((1,), (0,)), ((), ())), preferred_element_type=F32)


def fold8(v, op):
    return op(v.reshape(v.shape[0] // 8, 8, v.shape[1]), axis=0)


def kernel(
    q_hbm, k_hbm, v_hbm, g_hbm, len_ref, ord_ref,
    dq_ref, dk_ref, dv_ref,
    gk, gv, q_in, g_in, q_s, g_s, qn_s, gn_s, ksw, vsw, ktw, sbuf, pbuf, dsbuf, dkw, dvw,
    part_k, part_v, pair_k, pair_v, sum_k, sum_v, got_k, got_v, inv_vec, inv_ref,
    loc_sem, ag_send, ag_recv, rs_send, rs_recv,
):
    me = lax.axis_index("ctx")
    head = lax.axis_index("head")
    c = lax.rem(me, 2)
    x = lax.rem(lax.div(me, 2), RING)
    y = lax.div(me, 2 * RING)
    oc = 1 - c

    def wrap(v):
        return lax.rem(v, RING)

    xs = [wrap(x + d) for d in range(RING)]
    ys = [wrap(y + d) for d in range(RING)]

    def dev(yy, xx, cc):
        return ((yy * RING + xx) * 2 + cc, head)

    sib = dev(y, x, oc)

    own = []
    for i, (src, dst) in enumerate(((k_hbm, gk), (v_hbm, gv))):
        for h in range(2):
            rows = pl.ds(h * STRETCH, STRETCH)
            own.append(pltpu.make_async_copy(src.at[rows], dst.at[2 * me + h], loc_sem.at[2 * i + h]))
    loads = [
        pltpu.make_async_copy(q_hbm, q_in, loc_sem.at[4]),
        pltpu.make_async_copy(g_hbm, g_in, loc_sem.at[5]),
    ]
    for cp in own + loads:
        cp.start()

    barrier = pltpu.get_barrier_semaphore()
    peers = [dev(y, xs[d], c) for d in (1, 2, 3)] + [dev(ys[d], x, c) for d in (1, 2, 3)] + [sib]
    for peer in peers:
        pl.semaphore_signal(barrier, inc=1, device_id=peer, device_id_type=MESH)
    pl.semaphore_wait(barrier, len(peers))

    sent = []
    count = [0]

    def send(ref, to):
        k = count[0]
        count[0] += 1
        cp = pltpu.make_async_remote_copy(
            src_ref=ref, dst_ref=ref, send_sem=ag_send.at[k], recv_sem=ag_recv.at[k],
            device_id=to, device_id_type=MESH,
        )
        cp.start()
        sent.append(cp)
        return k

    def arrive(ref, k):
        pltpu.make_async_remote_copy(
            src_ref=ref, dst_ref=ref, send_sem=ag_send.at[k], recv_sem=ag_recv.at[k],
            device_id=sib, device_id_type=MESH,
        ).wait_recv()

    def block(yy, xx, cc):
        return ((yy * RING + xx) * 2 + cc) * 2

    def node(buf, yy, xx, cc):
        return buf.at[pl.ds(block(yy, xx, cc), 2)]

    def part_of(buf, yy, xx, cc, half):
        return buf.at[block(yy, xx, cc) + half]

    far_first, near_first = (2, 1, 3), (1, 3, 2)

    def first_stage(buf):
        mine = node(buf, y, x, c)
        along_x = {d: send(mine, dev(y, xs[d], c)) for d in far_first}
        along_y = {d: send(mine, dev(ys[d], x, c)) for d in far_first}
        return along_x, along_y, [(node(buf, y, x, oc), send(mine, sib))]

    def second_stage(buf, along_x, along_y, pending):
        coming = []
        for d in near_first:
            xx, yy = xs[RING - d], ys[RING - d]
            arrive(node(buf, y, xx, c), along_x[d])
            for e in far_first:
                k = send(part_of(buf, y, xx, c, 0), dev(ys[e], x, c))
                coming.append((e, ys[RING - e], xx, 0, k))
            arrive(node(buf, yy, x, c), along_y[d])
            for e in far_first:
                k = send(part_of(buf, yy, x, c, 1), dev(y, xs[e], c))
                coming.append((e, yy, xs[RING - e], 1, k))
            pending.append((node(buf, y, xx, oc), send(node(buf, y, xx, c), sib)))
            pending.append((node(buf, yy, x, oc), send(node(buf, yy, x, c), sib)))
        return coming

    def third_stage(buf, coming, pending):
        for e in near_first:
            for ee, yy, xx, half, k in coming:
                if ee == e:
                    arrive(part_of(buf, yy, xx, c, half), k)
                    pending.append((part_of(buf, yy, xx, oc, half), send(part_of(buf, yy, xx, c, half), sib)))

    lane = lax.broadcasted_iota(jnp.int32, (8, 128), 1)

    def invert_order():
        inv = jnp.zeros((8, 128), jnp.int32)
        for b in range(STRETCHES):
            inv = jnp.where(lane == ord_ref[b], b, inv)
        inv_vec[...] = inv
        cp = pltpu.make_async_copy(inv_vec, inv_ref, loc_sem.at[6])
        cp.start()
        return cp

    def stack_heads():
        for cp in loads:
            cp.wait()
        for a in range(2):
            for h in range(HEADS):
                src = (pl.ds(a * STRETCH, STRETCH), pl.ds(h * DIM, DIM))
                q_s[a, pl.ds(h * STRETCH, STRETCH), :] = q_in[src]
                g_s[a, pl.ds(h * STRETCH, STRETCH), :] = g_in[src]

    wait_k, wait_v = [], []
    for cp in own[:2]:
        cp.wait()
    k1 = first_stage(gk)
    for cp in own[2:]:
        cp.wait()
    v1 = first_stage(gv)
    inv_copy = invert_order()
    stack_heads()
    wait_k += k1[2]
    wait_v += v1[2]
    k2 = second_stage(gk, k1[0], k1[1], wait_k)
    v2 = second_stage(gv, v1[0], v1[1], wait_v)
    third_stage(gk, k2, wait_k)
    inv_copy.wait()

    spots, base = [], []
    for a in range(2):
        p = ord_ref[2 * me + a]
        spots.append(p)
        base.append(jnp.maximum(lax.div(p, 2) * 2 - 32, 0))

    scale = DIM ** -0.5
    log2e = 1.4426950408889634
    starts = [jnp.int32(0)]
    for d in range(3):
        starts.append(starts[-1] + len_ref[d])
    row_in = jnp.where(lane[:1] >= STRETCH, lane[:1] - STRETCH, lane[:1])
    pos_row, first_row = [], []
    for a in range(2):
        pr = spots[a] * STRETCH + row_in
        fr = jnp.zeros_like(pr)
        for st in starts:
            fr = jnp.maximum(fr, jnp.where(st <= pr, st, 0))
        pos_row.append(pr)
        first_row.append(fr)

    def window(src, dst):
        def step(w, carry):
            rows = pl.ds(pl.multiple_of(w * STRETCH, STRETCH), STRETCH)
            for a in range(2):
                dst[a, rows, :] = src[inv_ref[0, base[a] + w]]
            return carry

        lax.fori_loop(0, WIN, step, 0)

    for ref, k in wait_k:
        arrive(ref, k)
    window(gk, ksw)

    def score_step(j, carry):
        new = []
        for a in range(2):
            s = dot_nt(ksw[a, pl.ds(pl.multiple_of(j * KC, 16), KC), :], q_s[a])
            first_key = base[a] * STRETCH + j * KC
            kpos = first_key + lax.broadcasted_iota(jnp.int32, (KC, 128), 0)
            ok = (kpos <= pos_row[a]) & (kpos >= first_row[a])
            for g in range(GROUPS):
                cols = pl.ds(g * 128, 128)
                sg = jnp.where(ok, s[:, g * 128:(g + 1) * 128] * (scale * log2e), NEG)
                sbuf[a, pl.ds(pl.multiple_of(j * KC, 8), KC), cols] = sg
                new.append(jnp.maximum(carry[a * GROUPS + g], fold8(sg, jnp.max)))
        return tuple(new)

    tops = tuple(jnp.full((8, 128), NEG, F32) for _ in range(2 * GROUPS))
    tops = lax.fori_loop(0, WROWS // KC, score_step, tops)
    tops = [jnp.max(t, axis=0, keepdims=True) for t in tops]

    third_stage(gv, v2, wait_v)

    def weight_step(j, carry):
        new = []
        rows = pl.ds(pl.multiple_of(j * KC, 16), KC)
        for a in range(2):
            for g in range(GROUPS):
                cols = pl.ds(g * 128, 128)
                pw = jnp.exp2(sbuf[a, rows, cols] - tops[a * GROUPS + g])
                pbuf[a, rows, cols] = pw.astype(BF16)
                new.append(carry[a * GROUPS + g] + fold8(pw, jnp.sum))
        return tuple(new)

    zero = jnp.zeros((8, 128), F32)
    sums = tuple(zero for _ in range(2 * GROUPS))
    sums = lax.fori_loop(0, WROWS // KC, weight_step, sums)
    inv_l = [1.0 / jnp.sum(total, axis=0, keepdims=True) for total in sums]

    for a in range(2):
        for g in range(GROUPS):
            rows = pl.ds(g * 128, 128)
            col = jnp.broadcast_to(inv_l[a * GROUPS + g], (128, 128)).T
            qn_s[a, rows, :] = (q_s[a, rows, :].astype(F32) * (col * scale)).astype(BF16)
            gn_s[a, rows, :] = (g_s[a, rows, :].astype(F32) * col).astype(BF16)

    spans_of = KC // STRETCH

    def values_step(j, carry):
        rows = pl.ds(pl.multiple_of(j * KC, 16), KC)
        for a in range(2):
            dvw[a, pl.ds(j * spans_of, spans_of)] = dot_nn(pbuf[a, rows, :], gn_s[a]).reshape(spans_of, STRETCH, DIM)
        return carry

    lax.fori_loop(0, WROWS // KC, values_step, 0)
    for a in range(2):
        dkw[a, WIN] = jnp.zeros((STRETCH, DIM), F32)
        dvw[a, WIN] = jnp.zeros((STRETCH, DIM), F32)

    def rs_copy(src, dst, k, to):
        return pltpu.make_async_remote_copy(
            src_ref=src, dst_ref=dst, send_sem=rs_send.at[k], recv_sem=rs_recv.at[k],
            device_id=to, device_id_type=MESH,
        )

    def unsort(w, part, cc, k):
        def step(j, carry):
            chip = wrap(y + 2 + k) * RING + wrap(x + 2 + j)
            for half in range(2):
                s = ord_ref[2 * (2 * chip + cc) + half]
                at = []
                for a in range(2):
                    off = s - base[a]
                    at.append(jnp.where((off >= 0) & (off < WIN), off, WIN))
                part[cc, k, j, half] = (w[0, at[0]] + w[1, at[1]]).astype(BF16)
            return carry

        lax.fori_loop(0, RING, step, 0)

    def swap_start(w, part, pair, k0):
        cps = []
        for k in range(RING):
            unsort(w, part, oc, k)
            cp = rs_copy(part.at[oc, k], pair.at[k], k0 + k, sib)
            cp.start()
            cps.append(cp)
        for k in range(RING):
            unsort(w, part, c, k)
        return cps

    def scatter(part, pair, total, got, cps, k0):
        out = []
        for k in range(RING):
            cps[k].wait_recv()

            def step(j, carry):
                total[k, j] = (part[c, k, j].astype(F32) + pair[k, j].astype(F32)).astype(BF16)
                return carry

            lax.fori_loop(0, RING, step, 0)
            for j in range(RING):
                dy, dx = (2 + k) % RING, (2 + j) % RING
                if dy or dx:
                    cp = rs_copy(total.at[k, j], got.at[k, j], k0 + k * RING + j, dev(ys[dy], xs[dx], c))
                    cp.start()
                    out.append(cp)
        return out

    def collect(total, got, cps, out):
        for cp in cps:
            cp.wait_recv()
        for half in range(2):
            acc = total[2, 2, half].astype(F32)
            for k in range(RING):
                for j in range(RING):
                    if (k, j) != (2, 2):
                        acc = acc + got[k, j, half].astype(F32)
            out[pl.ds(half * STRETCH, STRETCH), :] = acc.astype(BF16)

    rs, swap_v, swap_k = [], [], []
    swap_v = swap_start(dvw, part_v, pair_v, 0)

    for ref, k in wait_v:
        arrive(ref, k)
    window(gv, vsw)

    def value_step(j, carry):
        new = []
        rows = pl.ds(pl.multiple_of(j * KC, 16), KC)
        for a in range(2):
            dp = dot_nt(vsw[a, rows, :], g_s[a])
            for g in range(GROUPS):
                cols = pl.ds(g * 128, 128)
                dpg = dp[:, g * 128:(g + 1) * 128]
                sbuf[a, rows, cols] = dpg
                new.append(carry[a * GROUPS + g] + fold8(pbuf[a, rows, cols].astype(F32) * dpg, jnp.sum))
        return tuple(new)

    sums = tuple(zero for _ in range(2 * GROUPS))
    sums = lax.fori_loop(0, WROWS // KC, value_step, sums)
    delta = [jnp.sum(t, axis=0, keepdims=True) * r for t, r in zip(sums, inv_l)]

    rs_v = []
    rs_v = scatter(part_v, pair_v, sum_v, got_v, swap_v, 8)

    def grad_step(j, carry):
        rows = pl.ds(pl.multiple_of(j * KC, 16), KC)
        for a in range(2):
            for g in range(GROUPS):
                cols = pl.ds(g * 128, 128)
                pw = pbuf[a, rows, cols].astype(F32)
                dsbuf[a, rows, cols] = (pw * (sbuf[a, rows, cols] - delta[a * GROUPS + g])).astype(BF16)
            dkw[a, pl.ds(j * spans_of, spans_of)] = dot_nn(dsbuf[a, rows, :], qn_s[a]).reshape(spans_of, STRETCH, DIM)
        return carry

    lax.fori_loop(0, WROWS // KC, grad_step, 0)

    swap_k = swap_start(dkw, part_k, pair_k, 4)
    rs_k = []
    rs_k = scatter(part_k, pair_k, sum_k, got_k, swap_k, 24)

    def turn_step(j, carry):
        rows = pl.ds(pl.multiple_of(j * 128, 128), 128)
        for a in range(2):
            ktw[a, :, rows] = ksw[a, rows, :].T
        return carry

    lax.fori_loop(0, WIN // 2, turn_step, 0)
    for a in range(2):
        dqt = dot_nn(ktw[a], dsbuf[a])
        for g in range(GROUPS):
            out = (dqt[:, g * 128:(g + 1) * 128] * (inv_l[a * GROUPS + g] * scale)).T.astype(BF16)
            for i in range(2):
                dq_ref[pl.ds(a * STRETCH, STRETCH), pl.ds((2 * g + i) * DIM, DIM)] = out[i * STRETCH:(i + 1) * STRETCH]

    collect(sum_v, got_v, rs_v, dv_ref)
    collect(sum_k, got_k, rs_k, dk_ref)
    for cp in sent + swap_v + swap_k + rs_v + rs_k:
        cp.wait_send()


def copy_out(*refs):
    for src, dst in zip(refs[:3], refs[3:]):
        dst[...] = src[...]


def body(queries, keys, values, grad_out, doc_lengths, stretch_order):
    anyspec = pl.BlockSpec(memory_space=pl.ANY)
    smem = pl.BlockSpec(memory_space=pltpu.SMEM)
    vmem = pl.BlockSpec(memory_space=pltpu.VMEM)
    half = (STRETCH, DIM)
    outs = tuple(jax.ShapeDtypeStruct(s.shape, BF16) for s in (queries, keys, values))
    grads = pl.pallas_call(
        kernel,
        out_shape=outs,
        in_specs=[anyspec] * 4 + [smem] * 2,
        out_specs=(vmem, vmem, vmem),
        scratch_shapes=[
            pltpu.VMEM((STRETCHES,) + half, BF16),
            pltpu.VMEM((STRETCHES,) + half, BF16),
            pltpu.VMEM((2 * STRETCH, HEADS * DIM), BF16),
            pltpu.VMEM((2 * STRETCH, HEADS * DIM), BF16),
            pltpu.VMEM((2, COLS, DIM), BF16),
            pltpu.VMEM((2, COLS, DIM), BF16),
            pltpu.VMEM((2, COLS, DIM), BF16),
            pltpu.VMEM((2, COLS, DIM), BF16),
            pltpu.VMEM((2, WROWS, DIM), BF16),
            pltpu.VMEM((2, WROWS, DIM), BF16),
            pltpu.VMEM((2, DIM, WROWS), BF16),
            pltpu.VMEM((2, WROWS, COLS), F32),
            pltpu.VMEM((2, WROWS, COLS), BF16),
            pltpu.VMEM((2, WROWS, COLS), BF16),
            pltpu.VMEM((2, WIN + 1) + half, F32),
            pltpu.VMEM((2, WIN + 1) + half, F32),
            pltpu.VMEM((2, RING, RING, 2) + half, BF16),
            pltpu.VMEM((2, RING, RING, 2) + half, BF16),
            pltpu.VMEM((RING, RING, 2) + half, BF16),
            pltpu.VMEM((RING, RING, 2) + half, BF16),
            pltpu.VMEM((RING, RING, 2) + half, BF16),
            pltpu.VMEM((RING, RING, 2) + half, BF16),
            pltpu.VMEM((RING, RING, 2) + half, BF16),
            pltpu.VMEM((RING, RING, 2) + half, BF16),
            pltpu.VMEM((8, 128), jnp.int32),
            pltpu.SMEM((8, 128), jnp.int32),
            pltpu.SemaphoreType.DMA((7,)),
            pltpu.SemaphoreType.DMA((N_AG,)),
            pltpu.SemaphoreType.DMA((N_AG,)),
            pltpu.SemaphoreType.DMA((N_RS,)),
            pltpu.SemaphoreType.DMA((N_RS,)),
        ],
        compiler_params=pltpu.CompilerParams(
            collective_id=0, has_side_effects=True, vmem_limit_bytes=58 * 1024 * 1024
        ),
    )(queries, keys, values, grad_out, doc_lengths, stretch_order)
    return pl.pallas_call(
        copy_out,
        out_shape=outs,
        in_specs=[vmem] * 3,
        out_specs=(vmem,) * 3,
    )(*grads)


def solution(mesh):
    return jax.shard_map(
        body,
        mesh=mesh,
        in_specs=(P("ctx", "head"), P("ctx", "head"), P("ctx", "head"), P("ctx", "head"), P(), P()),
        out_specs=(P("ctx", "head"), P("ctx", "head"), P("ctx", "head")),
        check_vma=False,
    )
```

time: 401 us -> 44.3 us (0.11)
  the two profiles are of different devices: /device:TPU:192 before, /device:TPU:1 now
where the time goes in v2:
time: 44.3 us; the launch traced here: 44.2 us
  Pallas kernels  43.5 us (98%)
  between operations  0.64 us (1%)
    pallas_call x1, Pallas kernels, body(): pl.pallas_call(kernel, out_shape=outs, in_specs=[anyspec] * 4 + [smem] *...  41.8 us
    pallas_call x1, Pallas kernels, body(): pl.pallas_call(copy_out, out_shape=outs, in_specs=[vmem] * 3, out_specs=(...  1.7 us

profile of v2, /device:TPU:1, one launch (start us, length us, event | category | flops | bytes accessed | tf_op | source)
XLA Modules:
  0.0 44.2 jit_solution(3352257662964275965)
XLA Ops:
  0.6 41.8 %shard_map.85 = (bf16[128,1024]{1,0:T(8,128)(2,1)}, bf16[128,128]{1,0:T(8,128)(2,1)}, bf16[128,128]{1,0:T(8,128)(2,1)}) custom-call(bf16[128,1024]{1,0:T(8,128)(2,1)} %q_hbm.1, bf16[128,128]{1,0:T(8,128)(2,1)} %k_hbm.1, bf16[128,128]{1,0:T(8,128)(2,1)} %v_hbm.1, bf16[128,1024]{1,0:T(8,128)(2,1)} %g_hbm.1, s32[4]{0:T(128)} %len_ref.1, s32[64]{0:T(128)} %ord_ref.1), custom_call_target="tpu_custom_call" | custom-call | tf_op jit(solution)/shard_map/pallas_call | solution.py:401
  42.5 1.7 %shard_map.86 = (bf16[128,1024]{1,0:T(8,128)(2,1)}, bf16[128,128]{1,0:T(8,128)(2,1)}, bf16[128,128]{1,0:T(8,128)(2,1)}) custom-call(bf16[128,1024]{1,0:T(8,128)(2,1)} %get-tuple-element.6.refs_0_, bf16[128,128]{1,0:T(8,128)(2,1)} %get-tuple-element.7.refs_1_, bf16[128,128]{1,0:T(8,128)(2,1)} %get-tuple-element.8.refs_2_), custom_call_target="tpu_custom_call" | custom-call | tf_op jit(solution)/shard_map/pallas_call | solution.py:443

commit v3 on v2

--- a/solution.py
+++ b/solution.py
@@ -21,7 +21,8 @@
 KC = 1088
 NEG = -1e30
 N_AG = 128
-N_RS = 48
+N_RS = 96
+HERE = 2
 
 
 def dot_nt(a, b):
@@ -40,7 +41,7 @@
     q_hbm, k_hbm, v_hbm, g_hbm, len_ref, ord_ref,
     dq_ref, dk_ref, dv_ref,
     gk, gv, q_in, g_in, q_s, g_s, qn_s, gn_s, ksw, vsw, ktw, sbuf, pbuf, dsbuf, dkw, dvw,
-    part_k, part_v, pair_k, pair_v, sum_k, sum_v, got_k, got_v, inv_vec, inv_ref,
+    part_k, part_v, pair_k, pair_v, sum_k, sum_v, got_k, got_v, mid_k, mid_v, last_k, last_v, inv_vec, inv_ref,
     loc_sem, ag_send, ag_recv, rs_send, rs_recv,
 ):
     me = lax.axis_index("ctx")
@@ -55,6 +56,7 @@
 
     xs = [wrap(x + d) for d in range(RING)]
     ys = [wrap(y + d) for d in range(RING)]
+    x2, y2 = xs[2], ys[2]
 
     def dev(yy, xx, cc):
         return ((yy * RING + xx) * 2 + cc, head)
@@ -108,7 +110,7 @@
     def part_of(buf, yy, xx, cc, half):
         return buf.at[block(yy, xx, cc) + half]
 
-    far_first, near_first = (2, 1, 3), (1, 3, 2)
+    far_first, near_first, group_order = (2, 1, 3), (1, 3, 2), (0, 1, 3, 2)
 
     def first_stage(buf):
         mine = node(buf, y, x, c)
@@ -121,19 +123,26 @@
         for d in near_first:
             xx, yy = xs[RING - d], ys[RING - d]
             arrive(node(buf, y, xx, c), along_x[d])
-            for e in far_first:
+            k = send(part_of(buf, y, xx, c, 0), dev(ys[2], x, c))
+            coming.append((2, y2, xx, 0, k))
+            arrive(node(buf, yy, x, c), along_y[d])
+            k = send(part_of(buf, yy, x, c, 1), dev(y, xs[2], c))
+            coming.append((2, yy, x2, 1, k))
+        for d in near_first:
+            xx, yy = xs[RING - d], ys[RING - d]
+            for e in (1, 3):
                 k = send(part_of(buf, y, xx, c, 0), dev(ys[e], x, c))
                 coming.append((e, ys[RING - e], xx, 0, k))
-            arrive(node(buf, yy, x, c), along_y[d])
-            for e in far_first:
                 k = send(part_of(buf, yy, x, c, 1), dev(y, xs[e], c))
                 coming.append((e, yy, xs[RING - e], 1, k))
+        for d in near_first:
+            xx, yy = xs[RING - d], ys[RING - d]
             pending.append((node(buf, y, xx, oc), send(node(buf, y, xx, c), sib)))
             pending.append((node(buf, yy, x, oc), send(node(buf, yy, x, c), sib)))
         return coming
 
     def third_stage(buf, coming, pending):
-        for e in near_first:
+        for e in far_first:
             for ee, yy, xx, half, k in coming:
                 if ee == e:
                     arrive(part_of(buf, yy, xx, c, half), k)
@@ -167,11 +176,11 @@
         cp.wait()
     v1 = first_stage(gv)
     inv_copy = invert_order()
-    stack_heads()
     wait_k += k1[2]
     wait_v += v1[2]
     k2 = second_stage(gk, k1[0], k1[1], wait_k)
     v2 = second_stage(gv, v1[0], v1[1], wait_v)
+    stack_heads()
     third_stage(gk, k2, wait_k)
     inv_copy.wait()
 
@@ -203,7 +212,7 @@
                 dst[a, rows, :] = src[inv_ref[0, base[a] + w]]
             return carry
 
-        lax.fori_loop(0, WIN, step, 0)
+        lax.fori_loop(0, WIN, step, 0, unroll=17)
 
     for ref, k in wait_k:
         arrive(ref, k)
@@ -227,8 +236,6 @@
     tops = lax.fori_loop(0, WROWS // KC, score_step, tops)
     tops = [jnp.max(t, axis=0, keepdims=True) for t in tops]
 
-    third_stage(gv, v2, wait_v)
-
     def weight_step(j, carry):
         new = []
         rows = pl.ds(pl.multiple_of(j * KC, 16), KC)
@@ -243,6 +250,7 @@
     zero = jnp.zeros((8, 128), F32)
     sums = tuple(zero for _ in range(2 * GROUPS))
     sums = lax.fori_loop(0, WROWS // KC, weight_step, sums)
+    third_stage(gv, v2, wait_v)
     inv_l = [1.0 / jnp.sum(total, axis=0, keepdims=True) for total in sums]
 
     for a in range(2):
@@ -254,13 +262,6 @@
 
     spans_of = KC // STRETCH
 
-    def values_step(j, carry):
-        rows = pl.ds(pl.multiple_of(j * KC, 16), KC)
-        for a in range(2):
-            dvw[a, pl.ds(j * spans_of, spans_of)] = dot_nn(pbuf[a, rows, :], gn_s[a]).reshape(spans_of, STRETCH, DIM)
-        return carry
-
-    lax.fori_loop(0, WROWS // KC, values_step, 0)
     for a in range(2):
         dkw[a, WIN] = jnp.zeros((STRETCH, DIM), F32)
         dvw[a, WIN] = jnp.zeros((STRETCH, DIM), F32)
@@ -271,61 +272,80 @@
             device_id=to, device_id_type=MESH,
         )
 
-    def unsort(w, part, cc, k):
-        def step(j, carry):
-            chip = wrap(y + 2 + k) * RING + wrap(x + 2 + j)
+    def unsort(w, part, cc, i):
+        def step(g, carry):
             for half in range(2):
+                dy, dx = (i, g) if half == 0 else (g, i)
+                chip = wrap(y + 2 + dy) * RING + wrap(x + 2 + dx)
                 s = ord_ref[2 * (2 * chip + cc) + half]
                 at = []
                 for a in range(2):
                     off = s - base[a]
                     at.append(jnp.where((off >= 0) & (off < WIN), off, WIN))
-                part[cc, k, j, half] = (w[0, at[0]] + w[1, at[1]]).astype(BF16)
+                part[cc, i, half, g] = (w[0, at[0]] + w[1, at[1]]).astype(BF16)
             return carry
 
-        lax.fori_loop(0, RING, step, 0)
+        lax.fori_loop(0, RING, step, 0, unroll=True)
 
     def swap_start(w, part, pair, k0):
-        cps = []
-        for k in range(RING):
-            unsort(w, part, oc, k)
-            cp = rs_copy(part.at[oc, k], pair.at[k], k0 + k, sib)
-            cp.start()
-            cps.append(cp)
-        for k in range(RING):
-            unsort(w, part, c, k)
+        cps = {}
+        for i in group_order:
+            unsort(w, part, oc, i)
+            cps[i] = rs_copy(part.at[oc, i], pair.at[i], k0 + i, sib)
+            cps[i].start()
         return cps
 
-    def scatter(part, pair, total, got, cps, k0):
+    def ring_peer(half, g):
+        return dev(y, xs[(2 + g) % RING], c) if half == 0 else dev(ys[(2 + g) % RING], x, c)
+
+    def scatter_rings(w, part, pair, total, got, cps, k0):
+        out = {}
+        for i in group_order:
+            unsort(w, part, c, i)
+            cps[i].wait_recv()
+            for g in group_order:
+                for half in range(2):
+                    both = part[c, i, half, g].astype(F32) + pair[i, half, g].astype(F32)
+                    total[i, half, g] = both.astype(BF16)
+                    if g != HERE:
+                        k = k0 + (i * 2 + half) * RING + g
+                        cp = rs_copy(total.at[i, half, g], got.at[i, half, g], k, ring_peer(half, g))
+                        cp.start()
+                        out[i, half, g] = cp
+        return out
+
+    def scatter_rest(total, got, mid, last, cps, k0):
         out = []
-        for k in range(RING):
-            cps[k].wait_recv()
-
-            def step(j, carry):
-                total[k, j] = (part[c, k, j].astype(F32) + pair[k, j].astype(F32)).astype(BF16)
-                return carry
-
-            lax.fori_loop(0, RING, step, 0)
-            for j in range(RING):
-                dy, dx = (2 + k) % RING, (2 + j) % RING
-                if dy or dx:
-                    cp = rs_copy(total.at[k, j], got.at[k, j], k0 + k * RING + j, dev(ys[dy], xs[dx], c))
+        for i in group_order:
+            for half in range(2):
+                acc = total[i, half, HERE].astype(F32)
+                for g in group_order[:3]:
+                    cps[i, half, g].wait_recv()
+                    acc = acc + got[i, half, g].astype(F32)
+                mid[half, i] = acc.astype(BF16)
+                if i != HERE:
+                    cp = rs_copy(mid.at[half, i], last.at[half, i], k0 + 2 * i + half, ring_peer(1 - half, i))
                     cp.start()
                     out.append(cp)
         return out
 
-    def collect(total, got, cps, out):
+    def collect_rest(mid, last, cps, out):
         for cp in cps:
             cp.wait_recv()
         for half in range(2):
-            acc = total[2, 2, half].astype(F32)
-            for k in range(RING):
-                for j in range(RING):
-                    if (k, j) != (2, 2):
-                        acc = acc + got[k, j, half].astype(F32)
+            acc = mid[half, HERE].astype(F32)
+            for i in group_order[:3]:
+                acc = acc + last[half, i].astype(F32)
             out[pl.ds(half * STRETCH, STRETCH), :] = acc.astype(BF16)
 
-    rs, swap_v, swap_k = [], [], []
+    swap_v, swap_k, rs_v, rs_v2, rs_k, rs_k2 = {}, {}, {}, [], {}, []
+    def values_step(j, carry):
+        rows = pl.ds(pl.multiple_of(j * KC, 16), KC)
+        for a in range(2):
+            dvw[a, pl.ds(j * spans_of, spans_of)] = dot_nn(pbuf[a, rows, :], gn_s[a]).reshape(spans_of, STRETCH, DIM)
+        return carry
+
+    lax.fori_loop(0, WROWS // KC, values_step, 0)
     swap_v = swap_start(dvw, part_v, pair_v, 0)
 
     for ref, k in wait_v:
@@ -348,8 +368,7 @@
     sums = lax.fori_loop(0, WROWS // KC, value_step, sums)
     delta = [jnp.sum(t, axis=0, keepdims=True) * r for t, r in zip(sums, inv_l)]
 
-    rs_v = []
-    rs_v = scatter(part_v, pair_v, sum_v, got_v, swap_v, 8)
+    rs_v = scatter_rings(dvw, part_v, pair_v, sum_v, got_v, swap_v, 8)
 
     def grad_step(j, carry):
         rows = pl.ds(pl.multiple_of(j * KC, 16), KC)
@@ -364,8 +383,8 @@
     lax.fori_loop(0, WROWS // KC, grad_step, 0)
 
     swap_k = swap_start(dkw, part_k, pair_k, 4)
-    rs_k = []
-    rs_k = scatter(part_k, pair_k, sum_k, got_k, swap_k, 24)
+
+    rs_k = scatter_rings(dkw, part_k, pair_k, sum_k, got_k, swap_k, 40)
 
     def turn_step(j, carry):
         rows = pl.ds(pl.multiple_of(j * 128, 128), 128)
@@ -374,22 +393,31 @@
         return carry
 
     lax.fori_loop(0, WIN // 2, turn_step, 0)
-    for a in range(2):
-        dqt = dot_nn(ktw[a], dsbuf[a])
-        for g in range(GROUPS):
-            out = (dqt[:, g * 128:(g + 1) * 128] * (inv_l[a * GROUPS + g] * scale)).T.astype(BF16)
-            for i in range(2):
-                dq_ref[pl.ds(a * STRETCH, STRETCH), pl.ds((2 * g + i) * DIM, DIM)] = out[i * STRETCH:(i + 1) * STRETCH]
-
-    collect(sum_v, got_v, rs_v, dv_ref)
-    collect(sum_k, got_k, rs_k, dk_ref)
-    for cp in sent + swap_v + swap_k + rs_v + rs_k:
+    def queries_out():
+        for a in range(2):
+            dqt = dot_nn(ktw[a], dsbuf[a])
+            for g in range(GROUPS):
+                out = (dqt[:, g * 128:(g + 1) * 128] * (inv_l[a * GROUPS + g] * scale)).T.astype(BF16)
+                for i in range(2):
+                    dq_ref[pl.ds(a * STRETCH, STRETCH), pl.ds((2 * g + i) * DIM, DIM)] = out[i * STRETCH:(i + 1) * STRETCH]
+
+    rs_v2 = scatter_rest(sum_v, got_v, mid_v, last_v, rs_v, 72)
+    queries_out()
+    rs_k2 = scatter_rest(sum_k, got_k, mid_k, last_k, rs_k, 80)
+    collect_rest(mid_v, last_v, rs_v2, dv_ref)
+    collect_rest(mid_k, last_k, rs_k2, dk_ref)
+    grouped = [cp for group in (swap_v, swap_k, rs_v, rs_k) for cp in group.values()]
+    for cp in sent + grouped + rs_v2 + rs_k2:
         cp.wait_send()
 
 
 def copy_out(*refs):
-    for src, dst in zip(refs[:3], refs[3:]):
-        dst[...] = src[...]
+    sem = refs[6]
+    cps = [pltpu.make_async_copy(refs[i], refs[i + 3], sem.at[i]) for i in range(3)]
+    for cp in cps:
+        cp.start()
+    for cp in cps:
+        cp.wait()
 
 
 def body(queries, keys, values, grad_out, doc_lengths, stretch_order):
@@ -398,10 +426,12 @@
     vmem = pl.BlockSpec(memory_space=pltpu.VMEM)
     half = (STRETCH, DIM)
     outs = tuple(jax.ShapeDtypeStruct(s.shape, BF16) for s in (queries, keys, values))
+    kept = tuple(pltpu.VMEM(s.shape, BF16) for s in outs)
+    hbm = pl.BlockSpec(memory_space=pltpu.HBM)
     grads = pl.pallas_call(
         kernel,
-        out_shape=outs,
-        in_specs=[anyspec] * 4 + [smem] * 2,
+        out_shape=kept,
+        in_specs=[hbm] * 4 + [smem] * 2,
         out_specs=(vmem, vmem, vmem),
         scratch_shapes=[
             pltpu.VMEM((STRETCHES,) + half, BF16),
@@ -420,14 +450,18 @@
             pltpu.VMEM((2, WROWS, COLS), BF16),
             pltpu.VMEM((2, WIN + 1) + half, F32),
             pltpu.VMEM((2, WIN + 1) + half, F32),
-            pltpu.VMEM((2, RING, RING, 2) + half, BF16),
-            pltpu.VMEM((2, RING, RING, 2) + half, BF16),
-            pltpu.VMEM((RING, RING, 2) + half, BF16),
-            pltpu.VMEM((RING, RING, 2) + half, BF16),
-            pltpu.VMEM((RING, RING, 2) + half, BF16),
-            pltpu.VMEM((RING, RING, 2) + half, BF16),
-            pltpu.VMEM((RING, RING, 2) + half, BF16),
-            pltpu.VMEM((RING, RING, 2) + half, BF16),
+            pltpu.VMEM((2, RING, 2, RING) + half, BF16),
+            pltpu.VMEM((2, RING, 2, RING) + half, BF16),
+            pltpu.VMEM((RING, 2, RING) + half, BF16),
+            pltpu.VMEM((RING, 2, RING) + half, BF16),
+            pltpu.VMEM((RING, 2, RING) + half, BF16),
+            pltpu.VMEM((RING, 2, RING) + half, BF16),
+            pltpu.VMEM((RING, 2, RING) + half, BF16),
+            pltpu.VMEM((RING, 2, RING) + half, BF16),
+            pltpu.VMEM((2, RING) + half, BF16),
+            pltpu.VMEM((2, RING) + half, BF16),
+            pltpu.VMEM((2, RING) + half, BF16),
+            pltpu.VMEM((2, RING) + half, BF16),
             pltpu.VMEM((8, 128), jnp.int32),
             pltpu.SMEM((8, 128), jnp.int32),
             pltpu.SemaphoreType.DMA((7,)),
@@ -444,8 +478,9 @@
         copy_out,
         out_shape=outs,
         in_specs=[vmem] * 3,
-        out_specs=(vmem,) * 3,
-    )(*grads)
+        out_specs=(hbm,) * 3,
+        scratch_shapes=[pltpu.SemaphoreType.DMA((3,))],
+    )(*(pltpu.with_memory_space_constraint(t, pltpu.VMEM) for t in grads))
 
 
 def solution(mesh):

time: 44.3 us -> 38.5 us (0.87)
  the two profiles are of different devices: /device:TPU:1 before, /device:TPU:192 now
where the time goes in v3:
time: 38.5 us; the launch traced here: 38.4 us
  Pallas kernels  37.8 us (98%)
  between operations  0.64 us (2%)
    pallas_call x1, Pallas kernels, body(): pl.pallas_call(kernel, out_shape=kept, in_specs=[hbm] * 4 + [smem] * 2, o...  37.1 us

profile of v3, /device:TPU:192, one launch (start us, length us, event | category | flops | bytes accessed | tf_op | source)
XLA Modules:
  0.0 38.4 jit_solution(4009411665446854700)
XLA Ops:
  0.6 37.1 %shard_map.85 = (bf16[128,1024]{1,0:T(8,128)(2,1)S(1)}, bf16[128,128]{1,0:T(8,128)(2,1)S(1)}, bf16[128,128]{1,0:T(8,128)(2,1)S(1)}) custom-call(bf16[128,1024]{1,0:T(8,128)(2,1)} %q_hbm.1, bf16[128,128]{1,0:T(8,128)(2,1)} %k_hbm.1, bf16[128,128]{1,0:T(8,128)(2,1)} %v_hbm.1, bf16[128,1024]{1,0:T(8,128)(2,1)} %g_hbm.1, s32[4]{0:T(128)} %len_ref.1, s32[64]{0:T(128)} %ord_ref.1), custom_call_target="tpu_custom_call" | custom-call | tf_op jit(solution)/shard_map/pallas_call | solution.py:431
  37.7 0.7 %shard_map.86 = (bf16[128,1024]{1,0:T(8,128)(2,1)}, bf16[128,128]{1,0:T(8,128)(2,1)}, bf16[128,128]{1,0:T(8,128)(2,1)}) custom-call(bf16[128,1024]{1,0:T(8,128)(2,1)S(1)} %get-tuple-element.6.refs_0_, bf16[128,128]{1,0:T(8,128)(2,1)S(1)} %get-tuple-element.7.refs_1_, bf16[128,128]{1,0:T(8,128)(2,1)S(1)} %get-tuple-element.8.refs_2_), custom_call_target="tpu_custom_call" | custom-call | tf_op jit(solution)/shard_map/pallas_call | solution.py:477

commit v4 on v3

--- a/solution.py
+++ b/solution.py
@@ -19,6 +19,8 @@
 WIN = 34
 WROWS = WIN * STRETCH
 KC = 1088
+ROWS = 128
+BLOCKS = WROWS // ROWS
 NEG = -1e30
 N_AG = 128
 N_RS = 96
@@ -63,6 +65,10 @@
 
     sib = dev(y, x, oc)
 
+    barrier = pltpu.get_barrier_semaphore()
+    peers = [dev(y, xs[d], c) for d in (1, 2, 3)] + [dev(ys[d], x, c) for d in (1, 2, 3)] + [sib]
+    for peer in peers:
+        pl.semaphore_signal(barrier, inc=1, device_id=peer, device_id_type=MESH)
     own = []
     for i, (src, dst) in enumerate(((k_hbm, gk), (v_hbm, gv))):
         for h in range(2):
@@ -75,10 +81,6 @@
     for cp in own + loads:
         cp.start()
 
-    barrier = pltpu.get_barrier_semaphore()
-    peers = [dev(y, xs[d], c) for d in (1, 2, 3)] + [dev(ys[d], x, c) for d in (1, 2, 3)] + [sib]
-    for peer in peers:
-        pl.semaphore_signal(barrier, inc=1, device_id=peer, device_id_type=MESH)
     pl.semaphore_wait(barrier, len(peers))
 
     sent = []
@@ -112,37 +114,41 @@
 
     far_first, near_first, group_order = (2, 1, 3), (1, 3, 2), (0, 1, 3, 2)
 
-    def first_stage(buf):
-        mine = node(buf, y, x, c)
-        along_x = {d: send(mine, dev(y, xs[d], c)) for d in far_first}
-        along_y = {d: send(mine, dev(ys[d], x, c)) for d in far_first}
-        return along_x, along_y, [(node(buf, y, x, oc), send(mine, sib))]
-
-    def second_stage(buf, along_x, along_y, pending):
+    def first_halves(buf):
+        along_x = {d: send(part_of(buf, y, x, c, 0), dev(y, xs[d], c)) for d in far_first}
+        along_y = {d: send(part_of(buf, y, x, c, 1), dev(ys[d], x, c)) for d in far_first}
+        return along_x, along_y
+
+    def other_halves(buf, pending):
+        along_x = {d: send(part_of(buf, y, x, c, 1), dev(y, xs[d], c)) for d in far_first}
+        along_y = {d: send(part_of(buf, y, x, c, 0), dev(ys[d], x, c)) for d in far_first}
+        pending.append((node(buf, y, x, oc), send(node(buf, y, x, c), sib)))
+        return along_x, along_y
+
+    def second_stage(buf, along_x, along_y):
         coming = []
         for d in near_first:
             xx, yy = xs[RING - d], ys[RING - d]
-            arrive(node(buf, y, xx, c), along_x[d])
-            k = send(part_of(buf, y, xx, c, 0), dev(ys[2], x, c))
-            coming.append((2, y2, xx, 0, k))
-            arrive(node(buf, yy, x, c), along_y[d])
-            k = send(part_of(buf, yy, x, c, 1), dev(y, xs[2], c))
-            coming.append((2, yy, x2, 1, k))
+            arrive(part_of(buf, y, xx, c, 0), along_x[d])
+            for e in far_first:
+                k = send(part_of(buf, y, xx, c, 0), dev(ys[e], x, c))
+                coming.append((e, ys[RING - e], xx, 0, k))
+            arrive(part_of(buf, yy, x, c, 1), along_y[d])
+            for e in far_first:
+                k = send(part_of(buf, yy, x, c, 1), dev(y, xs[e], c))
+                coming.append((e, yy, xs[RING - e], 1, k))
+        return coming
+
+    def share_first(buf, along_x, along_y, pending):
         for d in near_first:
             xx, yy = xs[RING - d], ys[RING - d]
-            for e in (1, 3):
-                k = send(part_of(buf, y, xx, c, 0), dev(ys[e], x, c))
-                coming.append((e, ys[RING - e], xx, 0, k))
-                k = send(part_of(buf, yy, x, c, 1), dev(y, xs[e], c))
-                coming.append((e, yy, xs[RING - e], 1, k))
-        for d in near_first:
-            xx, yy = xs[RING - d], ys[RING - d]
+            arrive(part_of(buf, y, xx, c, 1), along_x[d])
             pending.append((node(buf, y, xx, oc), send(node(buf, y, xx, c), sib)))
+            arrive(part_of(buf, yy, x, c, 0), along_y[d])
             pending.append((node(buf, yy, x, oc), send(node(buf, yy, x, c), sib)))
-        return coming
-
-    def third_stage(buf, coming, pending):
-        for e in far_first:
+
+    def share_second(buf, coming, pending, which):
+        for e in which:
             for ee, yy, xx, half, k in coming:
                 if ee == e:
                     arrive(part_of(buf, yy, xx, c, half), k)
@@ -171,17 +177,19 @@
     wait_k, wait_v = [], []
     for cp in own[:2]:
         cp.wait()
-    k1 = first_stage(gk)
+    k1 = first_halves(gk)
     for cp in own[2:]:
         cp.wait()
-    v1 = first_stage(gv)
+    v1 = first_halves(gv)
+    k1b = other_halves(gk, wait_k)
+    v1b = other_halves(gv, wait_v)
     inv_copy = invert_order()
-    wait_k += k1[2]
-    wait_v += v1[2]
-    k2 = second_stage(gk, k1[0], k1[1], wait_k)
-    v2 = second_stage(gv, v1[0], v1[1], wait_v)
+    k2 = second_stage(gk, *k1)
+    v2 = second_stage(gv, *v1)
+    share_first(gk, *k1b, wait_k)
     stack_heads()
-    third_stage(gk, k2, wait_k)
+    share_second(gk, k2, wait_k, near_first)
+    share_first(gv, *v1b, wait_v)
     inv_copy.wait()
 
     spots, base = [], []
@@ -218,53 +226,87 @@
         arrive(ref, k)
     window(gk, ksw)
 
-    def score_step(j, carry):
-        new = []
-        for a in range(2):
-            s = dot_nt(ksw[a, pl.ds(pl.multiple_of(j * KC, 16), KC), :], q_s[a])
-            first_key = base[a] * STRETCH + j * KC
-            kpos = first_key + lax.broadcasted_iota(jnp.int32, (KC, 128), 0)
+    def key_rows(i):
+        return pl.ds(i * ROWS, ROWS)
+
+    def scores(a):
+        tops = [jnp.full((8, 128), NEG, F32)] * GROUPS
+
+        def raise_tops(i):
+            for g in range(GROUPS):
+                tops[g] = jnp.maximum(tops[g], fold8(sbuf[a, key_rows(i), pl.ds(g * 128, 128)], jnp.max))
+
+        for i in range(BLOCKS):
+            s = dot_nt(ksw[a, key_rows(i), :], q_s[a])
+            kpos = base[a] * STRETCH + i * ROWS + lax.broadcasted_iota(jnp.int32, (ROWS, 128), 0)
             ok = (kpos <= pos_row[a]) & (kpos >= first_row[a])
             for g in range(GROUPS):
-                cols = pl.ds(g * 128, 128)
                 sg = jnp.where(ok, s[:, g * 128:(g + 1) * 128] * (scale * log2e), NEG)
-                sbuf[a, pl.ds(pl.multiple_of(j * KC, 8), KC), cols] = sg
-                new.append(jnp.maximum(carry[a * GROUPS + g], fold8(sg, jnp.max)))
-        return tuple(new)
-
-    tops = tuple(jnp.full((8, 128), NEG, F32) for _ in range(2 * GROUPS))
-    tops = lax.fori_loop(0, WROWS // KC, score_step, tops)
-    tops = [jnp.max(t, axis=0, keepdims=True) for t in tops]
-
-    def weight_step(j, carry):
-        new = []
-        rows = pl.ds(pl.multiple_of(j * KC, 16), KC)
+                sbuf[a, key_rows(i), pl.ds(g * 128, 128)] = sg
+            if i:
+                raise_tops(i - 1)
+        raise_tops(BLOCKS - 1)
+        return [jnp.max(t, axis=0, keepdims=True) for t in tops]
+
+    def weights(a, i, sums):
+        for g in range(GROUPS):
+            cols = pl.ds(g * 128, 128)
+            pw = jnp.exp2(sbuf[a, key_rows(i), cols] - tops[a][g])
+            pbuf[a, key_rows(i), cols] = pw.astype(BF16)
+            sums[g] = sums[g] + fold8(pw, jnp.sum)
+
+    def inverse_sums(a, sums):
+        for g in range(GROUPS):
+            inv_l.append(1.0 / jnp.sum(sums[g], axis=0, keepdims=True))
+
+    def column(a, g):
+        return jnp.broadcast_to(inv_l[a * GROUPS + g], (128, 128)).T
+
+    def scaled_grads(a):
+        for g in range(GROUPS):
+            rows = pl.ds(g * 128, 128)
+            gn_s[a, rows, :] = (g_s[a, rows, :].astype(F32) * column(a, g)).astype(BF16)
+
+    def scaled_queries():
         for a in range(2):
             for g in range(GROUPS):
-                cols = pl.ds(g * 128, 128)
-                pw = jnp.exp2(sbuf[a, rows, cols] - tops[a * GROUPS + g])
-                pbuf[a, rows, cols] = pw.astype(BF16)
-                new.append(carry[a * GROUPS + g] + fold8(pw, jnp.sum))
-        return tuple(new)
+                rows = pl.ds(g * 128, 128)
+                qn_s[a, rows, :] = (q_s[a, rows, :].astype(F32) * (column(a, g) * scale)).astype(BF16)
+
+    def value_grads(a, i):
+        part = dot_nn(pbuf[a, key_rows(i), :], gn_s[a])
+        dvw[a, pl.ds(i * (ROWS // STRETCH), ROWS // STRETCH)] = part.reshape(ROWS // STRETCH, STRETCH, DIM)
 
     zero = jnp.zeros((8, 128), F32)
-    sums = tuple(zero for _ in range(2 * GROUPS))
-    sums = lax.fori_loop(0, WROWS // KC, weight_step, sums)
-    third_stage(gv, v2, wait_v)
-    inv_l = [1.0 / jnp.sum(total, axis=0, keepdims=True) for total in sums]
-
+    tops, inv_l = [], []
     for a in range(2):
-        for g in range(GROUPS):
-            rows = pl.ds(g * 128, 128)
-            col = jnp.broadcast_to(inv_l[a * GROUPS + g], (128, 128)).T
-            qn_s[a, rows, :] = (q_s[a, rows, :].astype(F32) * (col * scale)).astype(BF16)
-            gn_s[a, rows, :] = (g_s[a, rows, :].astype(F32) * col).astype(BF16)
+        tops.append([jnp.zeros((1, 128), F32)] * GROUPS)
+    tops[0] = scores(0)
+    share_second(gv, v2, wait_v, near_first[:2])
+    tops[1] = scores(1)
+    share_second(gv, v2, wait_v, near_first[2:])
+    sums = [zero] * GROUPS
+    for i in range(BLOCKS):
+        weights(0, i, sums)
+    inverse_sums(0, sums)
+    scaled_grads(0)
+    sums = [zero] * GROUPS
+    for i in range(BLOCKS):
+        value_grads(0, i)
+        weights(1, i, sums)
+    inverse_sums(1, sums)
+    scaled_grads(1)
+    for i in range(BLOCKS):
+        value_grads(1, i)
 
     spans_of = KC // STRETCH
 
-    for a in range(2):
-        dkw[a, WIN] = jnp.zeros((STRETCH, DIM), F32)
-        dvw[a, WIN] = jnp.zeros((STRETCH, DIM), F32)
+    def spare_blocks():
+        for a in range(2):
+            dkw[a, WIN] = jnp.zeros((STRETCH, DIM), F32)
+            dvw[a, WIN] = jnp.zeros((STRETCH, DIM), F32)
+
+    spare_blocks()
 
     def rs_copy(src, dst, k, to):
         return pltpu.make_async_remote_copy(
@@ -339,35 +381,29 @@
             out[pl.ds(half * STRETCH, STRETCH), :] = acc.astype(BF16)
 
     swap_v, swap_k, rs_v, rs_v2, rs_k, rs_k2 = {}, {}, {}, [], {}, []
-    def values_step(j, carry):
-        rows = pl.ds(pl.multiple_of(j * KC, 16), KC)
-        for a in range(2):
-            dvw[a, pl.ds(j * spans_of, spans_of)] = dot_nn(pbuf[a, rows, :], gn_s[a]).reshape(spans_of, STRETCH, DIM)
-        return carry
-
-    lax.fori_loop(0, WROWS // KC, values_step, 0)
     swap_v = swap_start(dvw, part_v, pair_v, 0)
 
     for ref, k in wait_v:
         arrive(ref, k)
     window(gv, vsw)
 
-    def value_step(j, carry):
-        new = []
-        rows = pl.ds(pl.multiple_of(j * KC, 16), KC)
-        for a in range(2):
-            dp = dot_nt(vsw[a, rows, :], g_s[a])
-            for g in range(GROUPS):
-                cols = pl.ds(g * 128, 128)
-                dpg = dp[:, g * 128:(g + 1) * 128]
-                sbuf[a, rows, cols] = dpg
-                new.append(carry[a * GROUPS + g] + fold8(pbuf[a, rows, cols].astype(F32) * dpg, jnp.sum))
-        return tuple(new)
-
-    sums = tuple(zero for _ in range(2 * GROUPS))
-    sums = lax.fori_loop(0, WROWS // KC, value_step, sums)
-    delta = [jnp.sum(t, axis=0, keepdims=True) * r for t, r in zip(sums, inv_l)]
-
+    def weight_grads(a, i, sums):
+        dp = dot_nt(vsw[a, key_rows(i), :], g_s[a])
+        for g in range(GROUPS):
+            cols = pl.ds(g * 128, 128)
+            dpg = dp[:, g * 128:(g + 1) * 128]
+            sbuf[a, key_rows(i), cols] = dpg
+            sums[g] = sums[g] + fold8(pbuf[a, key_rows(i), cols].astype(F32) * dpg, jnp.sum)
+
+    dsums = []
+    for a in range(2):
+        sums = [zero] * GROUPS
+        for i in range(BLOCKS):
+            weight_grads(a, i, sums)
+        dsums += sums
+    delta = [jnp.sum(t, axis=0, keepdims=True) * r for t, r in zip(dsums, inv_l)]
+
+    scaled_queries()
     rs_v = scatter_rings(dvw, part_v, pair_v, sum_v, got_v, swap_v, 8)
 
     def grad_step(j, carry):
@@ -402,12 +438,15 @@
                     dq_ref[pl.ds(a * STRETCH, STRETCH), pl.ds((2 * g + i) * DIM, DIM)] = out[i * STRETCH:(i + 1) * STRETCH]
 
     rs_v2 = scatter_rest(sum_v, got_v, mid_v, last_v, rs_v, 72)
+    for cp in sent + list(swap_v.values()) + list(swap_k.values()) + list(rs_v.values()):
+        cp.wait_send()
     queries_out()
     rs_k2 = scatter_rest(sum_k, got_k, mid_k, last_k, rs_k, 80)
+    for cp in list(rs_k.values()) + rs_v2:
+        cp.wait_send()
     collect_rest(mid_v, last_v, rs_v2, dv_ref)
     collect_rest(mid_k, last_k, rs_k2, dk_ref)
-    grouped = [cp for group in (swap_v, swap_k, rs_v, rs_k) for cp in group.values()]
-    for cp in sent + grouped + rs_v2 + rs_k2:
+    for cp in rs_k2:
         cp.wait_send()
 
 

time: 38.5 us -> 38 us (0.987)
  Pallas kernels: 37.8 us -> 37.3 us
    pallas_call x1, Pallas kernels: 37.1 us -> 36.5 us  [body(): pl.pallas_call(kernel, out_shape=kept, in_specs=[hbm] * 4 + [smem] * 2, o...]
where the time goes in v4:
time: 38 us; the launch traced here: 37.9 us
  Pallas kernels  37.3 us (98%)
  between operations  0.64 us (2%)
    pallas_call x1, Pallas kernels, body(): pl.pallas_call(kernel, out_shape=kept, in_specs=[hbm] * 4 + [smem] * 2, o...  36.5 us

profile of v4, /device:TPU:192, one launch (start us, length us, event | category | flops | bytes accessed | tf_op | source)
XLA Modules:
  0.0 37.9 jit_solution(2323115371894908854)
XLA Ops:
  0.6 36.5 %shard_map.85 = (bf16[128,1024]{1,0:T(8,128)(2,1)S(1)}, bf16[128,128]{1,0:T(8,128)(2,1)S(1)}, bf16[128,128]{1,0:T(8,128)(2,1)S(1)}) custom-call(bf16[128,1024]{1,0:T(8,128)(2,1)} %q_hbm.1, bf16[128,128]{1,0:T(8,128)(2,1)} %k_hbm.1, bf16[128,128]{1,0:T(8,128)(2,1)} %v_hbm.1, bf16[128,1024]{1,0:T(8,128)(2,1)} %g_hbm.1, s32[4]{0:T(128)} %len_ref.1, s32[64]{0:T(128)} %ord_ref.1), custom_call_target="tpu_custom_call" | custom-call | tf_op jit(solution)/shard_map/pallas_call | solution.py:470
  37.2 0.7 %shard_map.86 = (bf16[128,1024]{1,0:T(8,128)(2,1)}, bf16[128,128]{1,0:T(8,128)(2,1)}, bf16[128,128]{1,0:T(8,128)(2,1)}) custom-call(bf16[128,1024]{1,0:T(8,128)(2,1)S(1)} %get-tuple-element.6.refs_0_, bf16[128,128]{1,0:T(8,128)(2,1)S(1)} %get-tuple-element.7.refs_1_, bf16[128,128]{1,0:T(8,128)(2,1)S(1)} %get-tuple-element.8.refs_2_), custom_call_target="tpu_custom_call" | custom-call | tf_op jit(solution)/shard_map/pallas_call | solution.py:516

commit v5 on v4

--- a/solution.py
+++ b/solution.py
@@ -21,6 +21,8 @@
 KC = 1088
 ROWS = 128
 BLOCKS = WROWS // ROWS
+WIDE = 272
+WIDES = WROWS // WIDE
 NEG = -1e30
 N_AG = 128
 N_RS = 96
@@ -229,30 +231,33 @@
     def key_rows(i):
         return pl.ds(i * ROWS, ROWS)
 
+    def wide_rows(i):
+        return pl.ds(i * WIDE, WIDE)
+
     def scores(a):
         tops = [jnp.full((8, 128), NEG, F32)] * GROUPS
 
         def raise_tops(i):
             for g in range(GROUPS):
-                tops[g] = jnp.maximum(tops[g], fold8(sbuf[a, key_rows(i), pl.ds(g * 128, 128)], jnp.max))
-
-        for i in range(BLOCKS):
-            s = dot_nt(ksw[a, key_rows(i), :], q_s[a])
-            kpos = base[a] * STRETCH + i * ROWS + lax.broadcasted_iota(jnp.int32, (ROWS, 128), 0)
+                tops[g] = jnp.maximum(tops[g], fold8(sbuf[a, wide_rows(i), pl.ds(g * 128, 128)], jnp.max))
+
+        for i in range(WIDES):
+            s = dot_nt(ksw[a, wide_rows(i), :], q_s[a])
+            kpos = base[a] * STRETCH + i * WIDE + lax.broadcasted_iota(jnp.int32, (WIDE, 128), 0)
             ok = (kpos <= pos_row[a]) & (kpos >= first_row[a])
             for g in range(GROUPS):
                 sg = jnp.where(ok, s[:, g * 128:(g + 1) * 128] * (scale * log2e), NEG)
-                sbuf[a, key_rows(i), pl.ds(g * 128, 128)] = sg
+                sbuf[a, wide_rows(i), pl.ds(g * 128, 128)] = sg
             if i:
                 raise_tops(i - 1)
-        raise_tops(BLOCKS - 1)
+        raise_tops(WIDES - 1)
         return [jnp.max(t, axis=0, keepdims=True) for t in tops]
 
     def weights(a, i, sums):
         for g in range(GROUPS):
             cols = pl.ds(g * 128, 128)
-            pw = jnp.exp2(sbuf[a, key_rows(i), cols] - tops[a][g])
-            pbuf[a, key_rows(i), cols] = pw.astype(BF16)
+            pw = jnp.exp2(sbuf[a, wide_rows(i), cols] - tops[a][g])
+            pbuf[a, wide_rows(i), cols] = pw.astype(BF16)
             sums[g] = sums[g] + fold8(pw, jnp.sum)
 
     def inverse_sums(a, sums):
@@ -274,9 +279,10 @@
                 qn_s[a, rows, :] = (q_s[a, rows, :].astype(F32) * (column(a, g) * scale)).astype(BF16)
 
     def value_grads(a, i):
-        part = dot_nn(pbuf[a, key_rows(i), :], gn_s[a])
-        dvw[a, pl.ds(i * (ROWS // STRETCH), ROWS // STRETCH)] = part.reshape(ROWS // STRETCH, STRETCH, DIM)
-
+        part = dot_nn(pbuf[a, pl.ds(i * KC, KC), :], gn_s[a])
+        dvw[a, pl.ds(i * spans_of, spans_of)] = part.reshape(spans_of, STRETCH, DIM)
+
+    spans_of = KC // STRETCH
     zero = jnp.zeros((8, 128), F32)
     tops, inv_l = [], []
     for a in range(2):
@@ -286,18 +292,18 @@
     tops[1] = scores(1)
     share_second(gv, v2, wait_v, near_first[2:])
     sums = [zero] * GROUPS
-    for i in range(BLOCKS):
+    for i in range(WIDES):
         weights(0, i, sums)
     inverse_sums(0, sums)
     scaled_grads(0)
     sums = [zero] * GROUPS
-    for i in range(BLOCKS):
-        value_grads(0, i)
+    for i in range(WIDES):
         weights(1, i, sums)
     inverse_sums(1, sums)
     scaled_grads(1)
-    for i in range(BLOCKS):
-        value_grads(1, i)
+    for a in range(2):
+        for i in range(WROWS // KC):
+            value_grads(a, i)
 
     spans_of = KC // STRETCH
 
@@ -388,17 +394,17 @@
     window(gv, vsw)
 
     def weight_grads(a, i, sums):
-        dp = dot_nt(vsw[a, key_rows(i), :], g_s[a])
+        dp = dot_nt(vsw[a, wide_rows(i), :], g_s[a])
         for g in range(GROUPS):
             cols = pl.ds(g * 128, 128)
             dpg = dp[:, g * 128:(g + 1) * 128]
-            sbuf[a, key_rows(i), cols] = dpg
-            sums[g] = sums[g] + fold8(pbuf[a, key_rows(i), cols].astype(F32) * dpg, jnp.sum)
+            sbuf[a, wide_rows(i), cols] = dpg
+            sums[g] = sums[g] + fold8(pbuf[a, wide_rows(i), cols].astype(F32) * dpg, jnp.sum)
 
     dsums = []
     for a in range(2):
         sums = [zero] * GROUPS
-        for i in range(BLOCKS):
+        for i in range(WIDES):
             weight_grads(a, i, sums)
         dsums += sums
     delta = [jnp.sum(t, axis=0, keepdims=True) * r for t, r in zip(dsums, inv_l)]

time: 38 us -> 37.5 us (0.987)
  Pallas kernels: 37.3 us -> 36.8 us
    pallas_call x1, Pallas kernels: 36.5 us -> 36.1 us  [body(): pl.pallas_call(kernel, out_shape=kept, in_specs=[hbm] * 4 + [smem] * 2, o...]
where the time goes in v5:
time: 37.5 us; the launch traced here: 37.4 us
  Pallas kernels  36.8 us (98%)
  between operations  0.64 us (2%)
    pallas_call x1, Pallas kernels, body(): pl.pallas_call(kernel, out_shape=kept, in_specs=[hbm] * 4 + [smem] * 2, o...  36.1 us

profile of v5, /device:TPU:192, one launch (start us, length us, event | category | flops | bytes accessed | tf_op | source)
XLA Modules:
  0.0 37.4 jit_solution(12244062192710111027)
XLA Ops:
  0.6 36.1 %shard_map.85 = (bf16[128,1024]{1,0:T(8,128)(2,1)S(1)}, bf16[128,128]{1,0:T(8,128)(2,1)S(1)}, bf16[128,128]{1,0:T(8,128)(2,1)S(1)}) custom-call(bf16[128,1024]{1,0:T(8,128)(2,1)} %q_hbm.1, bf16[128,128]{1,0:T(8,128)(2,1)} %k_hbm.1, bf16[128,128]{1,0:T(8,128)(2,1)} %v_hbm.1, bf16[128,1024]{1,0:T(8,128)(2,1)} %g_hbm.1, s32[4]{0:T(128)} %len_ref.1, s32[64]{0:T(128)} %ord_ref.1), custom_call_target="tpu_custom_call" | custom-call | tf_op jit(solution)/shard_map/pallas_call | solution.py:476
  36.7 0.7 %shard_map.86 = (bf16[128,1024]{1,0:T(8,128)(2,1)}, bf16[128,128]{1,0:T(8,128)(2,1)}, bf16[128,128]{1,0:T(8,128)(2,1)}) custom-call(bf16[128,1024]{1,0:T(8,128)(2,1)S(1)} %get-tuple-element.6.refs_0_, bf16[128,128]{1,0:T(8,128)(2,1)S(1)} %get-tuple-element.7.refs_1_, bf16[128,128]{1,0:T(8,128)(2,1)S(1)} %get-tuple-element.8.refs_2_), custom_call_target="tpu_custom_call" | custom-call | tf_op jit(solution)/shard_map/pallas_call | solution.py:522

commit v6 on v5

--- a/solution.py
+++ b/solution.py
@@ -422,7 +422,7 @@
             dkw[a, pl.ds(j * spans_of, spans_of)] = dot_nn(dsbuf[a, rows, :], qn_s[a]).reshape(spans_of, STRETCH, DIM)
         return carry
 
-    lax.fori_loop(0, WROWS // KC, grad_step, 0)
+    lax.fori_loop(0, WROWS // KC, grad_step, 0, unroll=True)
 
     swap_k = swap_start(dkw, part_k, pair_k, 4)
 

time: 37.5 us -> 37.4 us (level)
  no operation moved by 1% of the time
where the time goes in v6:
time: 37.4 us; the launch traced here: 37.3 us
  Pallas kernels  36.7 us (98%)
  between operations  0.64 us (2%)
    pallas_call x1, Pallas kernels, body(): pl.pallas_call(kernel, out_shape=kept, in_specs=[hbm] * 4 + [smem] * 2, o...  36 us

profile of v6, /device:TPU:192, one launch (start us, length us, event | category | flops | bytes accessed | tf_op | source)
XLA Modules:
  0.0 37.3 jit_solution(13696150042715156668)
XLA Ops:
  0.6 36.0 %shard_map.85 = (bf16[128,1024]{1,0:T(8,128)(2,1)S(1)}, bf16[128,128]{1,0:T(8,128)(2,1)S(1)}, bf16[128,128]{1,0:T(8,128)(2,1)S(1)}) custom-call(bf16[128,1024]{1,0:T(8,128)(2,1)} %q_hbm.1, bf16[128,128]{1,0:T(8,128)(2,1)} %k_hbm.1, bf16[128,128]{1,0:T(8,128)(2,1)} %v_hbm.1, bf16[128,1024]{1,0:T(8,128)(2,1)} %g_hbm.1, s32[4]{0:T(128)} %len_ref.1, s32[64]{0:T(128)} %ord_ref.1), custom_call_target="tpu_custom_call" | custom-call | tf_op jit(solution)/shard_map/pallas_call | solution.py:476
  36.6 0.7 %shard_map.86 = (bf16[128,1024]{1,0:T(8,128)(2,1)}, bf16[128,128]{1,0:T(8,128)(2,1)}, bf16[128,128]{1,0:T(8,128)(2,1)}) custom-call(bf16[128,1024]{1,0:T(8,128)(2,1)S(1)} %get-tuple-element.6.refs_0_, bf16[128,128]{1,0:T(8,128)(2,1)S(1)} %get-tuple-element.7.refs_1_, bf16[128,128]{1,0:T(8,128)(2,1)S(1)} %get-tuple-element.8.refs_2_), custom_call_target="tpu_custom_call" | custom-call | tf_op jit(solution)/shard_map/pallas_call | solution.py:522
